TPU v7x, 512 devices: a whole 4x4x16 slice. The times are simulated.
512 devices in a mesh: bank: 128 (over x, z_lo, y), det: 4 (over z_hi, core).
Axes of the slice: x: 4, y: 4, z: 16 (z_hi: 2, z_lo: 8; z = z_hi * 8 + z_lo), core: 2. Of those that a mesh axis runs over, the one named last changes fastest.
Arguments:
- strain: float32 [4, 256, 2, 256], P('det', 'bank'), may hold values from -4 to 4
- inverse_noise: float32 [4, 256, 256], P('det', 'bank'), may hold values from 0.4 to 4
- slides: int32 [4], P('det'), may hold values from 0 to 131071
- templates: float32 [512, 256, 2, 256], P(('bank', 'det')), may hold values from -6 to 6
- cutoffs: int32 [512], P(('bank', 'det')), may hold values from 16384 to 65536
Outputs:
- loudest: float32 [131072], P('bank')
- network: float32 [512, 131072], P(('bank', 'det'))
All inputs are finite; a program needn't handle non-finite values.
Results may differ from a plain program's by a relative error of at most 0.0003.
Values sent between devices are 32-bit elements; how exact they have to be, the bound alone decides.
No kernel may reach another device: no remote copies, remote signals or barrier semaphores. Data moves between devices by JAX's collectives and lax.ppermute only.
A program may use at most 64 MiB of HBM per device.

v0:
```python
import math

import jax
import jax.numpy as jnp
from jax import lax
from jax.sharding import PartitionSpec as P

highest = lax.Precision.HIGHEST


def contract(form, left, right):
    return jnp.einsum(form, left, right, precision=highest)


def tables(rows, cols):
    span = 2 * rows
    total = span * cols
    row_ids = jnp.arange(rows, dtype=jnp.int32)
    time_ids = jnp.arange(span, dtype=jnp.int32)
    col_ids = jnp.arange(cols, dtype=jnp.int32)
    first = (row_ids[:, None] * time_ids[None, :] % span).astype(jnp.float32) * (
        2.0 * math.pi / span
    )
    turn = (col_ids[:, None] * time_ids[None, :]).astype(jnp.float32) * (2.0 * math.pi / total)
    last = (col_ids[:, None] * col_ids[None, :] % cols).astype(jnp.float32) * (2.0 * math.pi / cols)
    return (
        jnp.cos(first),
        jnp.sin(first),
        jnp.cos(turn),
        jnp.sin(turn),
        jnp.cos(last),
        jnp.sin(last),
    )


def accumulate(pieces, templates, cutoffs, first_cos, first_sin):
    piece_strain, piece_noise = pieces
    count = piece_noise.shape[1]
    cols = piece_noise.shape[2]
    row_ids = jnp.arange(count, dtype=jnp.int32)
    bin_ids = row_ids[:, None] * cols + jnp.arange(cols, dtype=jnp.int32)[None, :]
    bin_mask = (bin_ids[None, :, :] < cutoffs[:, None, None]).astype(jnp.float32)
    weight = piece_noise[None, :, :, :] * bin_mask[:, None, :, :]
    wave_re = templates[:, None, :, 0, :]
    wave_im = templates[:, None, :, 1, :]
    data_re = piece_strain[None, :, :, 0, :]
    data_im = piece_strain[None, :, :, 1, :]
    prod_re = (data_re * wave_re + data_im * wave_im) * weight
    prod_im = (data_im * wave_re - data_re * wave_im) * weight
    energy = jnp.sum((wave_re * wave_re + wave_im * wave_im) * weight, axis=(2, 3))
    section_re = contract("tdrc,rn->tdcn", prod_re, first_cos) - contract(
        "tdrc,rn->tdcn", prod_im, first_sin
    )
    section_im = contract("tdrc,rn->tdcn", prod_re, first_sin) + contract(
        "tdrc,rn->tdcn", prod_im, first_cos
    )
    return (section_re, section_im, energy)


def finish(carry, all_slides, turn_cos, turn_sin, last_cos, last_sin):
    section_re, section_im, energy = carry
    twist_re = section_re * turn_cos - section_im * turn_sin
    twist_im = section_re * turn_sin + section_im * turn_cos
    out_re = contract("mc,tdcn->tdmn", last_cos, twist_re) - contract(
        "mc,tdcn->tdmn", last_sin, twist_im
    )
    out_im = contract("mc,tdcn->tdmn", last_sin, twist_re) + contract(
        "mc,tdcn->tdmn", last_cos, twist_im
    )
    power = (out_re * out_re + out_im * out_im) / energy[:, :, None, None]
    count, detectors = energy.shape
    power = power.reshape(count, detectors, -1)
    network = jnp.roll(power[:, 0], -all_slides[0], axis=1)
    for index in range(1, detectors):
        network = network + jnp.roll(power[:, index], -all_slides[index], axis=1)
    return network


def shards(strain, inverse_noise, slides, templates, cutoffs):
    banks = lax.axis_size("bank")
    rows = strain.shape[1] * banks
    cols = strain.shape[3]
    first_cos, first_sin, turn_cos, turn_sin, last_cos, last_sin = tables(rows, cols)
    row_strain, row_noise = (
        lax.all_gather(strain, "bank", axis=1, tiled=True),
        lax.all_gather(inverse_noise, "bank", axis=1, tiled=True),
    )
    full_strain, full_noise, all_slides = (
        lax.all_gather(row_strain, "det", axis=0, tiled=True),
        lax.all_gather(row_noise, "det", axis=0, tiled=True),
        lax.all_gather(slides, "det", axis=0, tiled=True),
    )
    carry = accumulate((full_strain, full_noise), templates, cutoffs, first_cos, first_sin)
    network = finish(carry, all_slides, turn_cos, turn_sin, last_cos, last_sin)
    peak = jnp.max(network, axis=0)
    block = peak.shape[0] // banks
    whole = lax.pmax(peak, ("bank", "det"))
    loudest = lax.dynamic_slice_in_dim(whole, lax.axis_index("bank") * block, block)
    return (loudest, network)


def solution(mesh):
    return jax.shard_map(
        shards,
        mesh=mesh,
        in_specs=(
            P("det", "bank", None, None),
            P("det", "bank", None),
            P("det"),
            P(("bank", "det"), None, None, None),
            P(("bank", "det")),
        ),
        out_specs=(P("bank"), P(("bank", "det"), None)),
        check_vma=False,
    )
```

profile of v0, /device:TPU:1, one launch (start us, length us, event | category | flops | bytes accessed | tf_op | source)
XLA Modules:
  0.0 1655.9 jit_solution(8012002461764196452)
XLA Ops:
  7.2 494.7 %all_gather.15 = f32[1,256,2,256]{3,2,0,1:T(2,128)} all-gather(f32[1,2,2,256]{3,2,0,1:T(2,128)} %bitcast.75), channel_id=1, replica_groups=mesh['bank'=128,'det'=4] {'bank'}, dimensions={1}, use_global_device_ids=true | all-gather | bytes 528384 | tf_op jit(solution)/shard_map/all_gather | solution.py:85
  501.9 0.0 all-gather.5.cloned.1.call-start
  502.0 0.7 copy.33
  502.6 467.6 %all_gather.17 = f32[1,256,256]{2,0,1:T(1,128)S(1)} all-gather(f32[1,2,256]{2,0,1:T(1,128)S(1)} %copy.33), channel_id=1, replica_groups=mesh['bank'=128,'det'=4] {'bank'}, dimensions={1}, use_global_device_ids=true | all-gather | bytes 264192 | tf_op jit(solution)/shard_map/all_gather | solution.py:86
  970.3 0.7 copy.34
  971.7 1.3 dynamic-slice
  972.9 0.8 dynamic-update-slice
  973.8 119.2 %all-reduce = s32[4]{0:T(128)S(1)} all-reduce(s32[4]{0:T(128)S(1)} %dynamic-update-slice), channel_id=1, replica_groups=mesh['bank'=128,'det'=4] {'det'}, use_global_device_ids=true, to_apply=%add | all-reduce | flops 4 | bytes 32
  1093.0 0.6 fusion.83
  1096.8 1.9 fusion.18
  1098.7 0.8 fusion.42
  1099.5 0.4 fusion.82
  1100.0 0.8 copy_bitcast_fusion.1
  1100.8 5.0 fusion.81
  1105.8 25.3 %all-gather.5.cloned.1.call-done = f32[4,256,256]{2,1,0:T(8,128)} async-done(((f32[1,256,256]{2,1,0:T(8,128)}), f32[4,256,256]{2,1,0:T(8,128)}) %all-gather.5.cloned.1.call-update) | async-done | bytes 1048592 | tf_op jit(solution)/shard_map/all_gather | solution.py:90
  1131.1 4.9 fusion.4
  1136.0 1.6 copy.36
  1137.6 5.0 fusion.16
  1142.6 5.0 fusion.12
  1147.6 0.4 copy.37
  1148.0 5.8 convolution_subtract_fusion
  1153.8 4.6 convolution_add_fusion
  1158.4 4.4 fusion.28
  1162.8 4.4 fusion.31
  1167.2 4.8 fusion.26
  1172.0 4.6 fusion
  1176.6 1.9 copy.44
  1178.5 3.0 reshape.158
  1181.5 1.5 slice_bitcast_fusion
  1183.1 15.4 add_add_fusion
  1198.5 449.4 %all-reduce.3.cloned.1.call-done = f32[131072]{0:T(1024)} async-done(((f32[131072]{0:T(1024)}), f32[131072]{0:T(1024)}) %all-reduce.3.cloned.1.call-update) | async-done | bytes 524304 | tf_op jit(solution)/shard_map/pmax | solution.py:97
  1647.9 1.3 dynamic_slice.6
  (13 shorter events, 0.2 us)
Async XLA Ops:
  7.2 1092.4 %copy-start.1 = (f32[1,256,2,256]{3,2,1,0:T(2,128)S(1)}, f32[1,256,2,256]{3,2,1,0:T(2,128)}, u32[]{:S(2)}) copy-start(f32[1,256,2,256]{3,2,1,0:T(2,128)} %param.10) | copy-start | bytes 1572868
  7.2 1093.6 %all-gather.3.cloned.1.call-start = ((), (), s32[]{:S(2)}) async-start(), calls=%async_computation | async-start | bytes 2621440 | tf_op jit(solution)/shard_map/all_gather | solution.py:89
  501.9 629.2 %all-gather.5.cloned.1.call-start = ((), (), s32[]{:S(2)}) async-start(), calls=%async_computation.1 | async-start | bytes 1310720 | tf_op jit(solution)/shard_map/all_gather | solution.py:90
  973.7 674.2 %all-reduce.3.cloned.1.call-start = ((), (), s32[]{:S(2)}) async-start(), calls=%async_computation.2 | async-start | bytes 1048576 | tf_op jit(solution)/shard_map/pmax | solution.py:97
  1148.0 5.8 copy-start
Sparse Core Ops, SparseCore 0:
  502.0 124.2 all-gather.2
  973.8 157.2 all-gather.4
  1198.6 449.2 all-reduce.2
where the time goes:
time: 1660 us
  blocking collectives  1080 us (65%)
  waiting for transfers between devices  475 us (29%)
  matrix products  38.6 us (2%)
  other arithmetic  23 us (1%)
  local copies, waits for them, and re-layouts  19.9 us (1%)
  between operations  18 us (1%)
    all_gather x1, blocking collectives, shards(): lax.all_gather(strain, 'bank', axis=1, tiled=True)  495 us
    all_gather x1, blocking collectives, shards(): lax.all_gather(inverse_noise, 'bank', axis=1, tiled=True)  468 us
    pmax x1, waiting for transfers between devices, shards(): whole = lax.pmax(peak, ('bank', 'det'))  449 us
    unnamed x1, blocking collectives  119 us
    dot_general x8, matrix products, contract(): return jnp.einsum(form, left, right, precision=highest)  38.6 us
  transfers between devices with their start and end apart: 3, of which 2 were waited for; matrix products, arithmetic and copies ran while one was open for 1% of the time, Pallas kernels for 0%

commit v1 on v0

v1 whole, which is shorter than its diff:
```python
import jax
import jax.numpy as jnp
import ml_dtypes
import numpy as np
from jax import lax
from jax.experimental import pallas as pl
from jax.experimental.pallas import tpu as pltpu
from jax.sharding import Mesh, PartitionSpec as P

ROWS = 256
COLS = 256
SPAN = 512
SERIES = 131072
PLANE = ("x", "y")
PILE = ("zl", "zh")
CHIP = ("x", "y", "core")
STACK = ("zl", "zh", "core")


def split(values):
    high = values.astype(ml_dtypes.bfloat16)
    low = (values - high.astype(np.float64)).astype(ml_dtypes.bfloat16)
    return np.stack([high, low])


def plane_order():
    slot = np.arange(128)
    return slot // 32, slot // 8 % 4, slot % 8


def tables():
    x, y, zl = plane_order()
    first = []
    for parity in range(2):
        row = x * 64 + zl * 8 + y * 2 + parity
        angle = 2.0 * np.pi * (np.arange(256)[:, None] * row[None, :] % SPAN) / SPAN
        cos, sin = np.cos(angle), np.sin(angle)
        whole = []
        for chunk in range(2):
            part = slice(chunk * 128, chunk * 128 + 128)
            whole.append(np.block([[cos[part], -sin[part]], [sin[part], cos[part]]]))
        first.append(split(np.concatenate(whole)))
    first = np.stack(first)
    angle = 2.0 * np.pi * (np.arange(SPAN)[:, None] * np.arange(COLS)[None, :]) / SERIES
    turn = np.stack([np.cos(angle), np.sin(angle)]).astype(np.float32)
    last = []
    for parity in range(2):
        m = 2 * (x * 32 + zl * 4 + y) + parity
        angle = 2.0 * np.pi * (np.arange(128)[:, None] * m[None, :] % COLS) / COLS
        cos, sin = np.cos(angle), np.sin(angle)
        last.append(split(np.block([[cos, sin], [-sin, cos]])))
    return first, turn, np.stack(last)


def dot(left, right):
    return jnp.dot(left, right, preferred_element_type=jnp.float32)


def halves(value):
    high = value.astype(jnp.bfloat16)
    low = (value - high.astype(jnp.float32)).astype(jnp.bfloat16)
    return high, low


def kernel(
    cutoff_ref,
    wave_ref,
    mine_ref,
    other_ref,
    first_ref,
    turn_ref,
    last_ref,
    network_ref,
    loud_ref,
    masked,
    squares,
    piece,
    total,
):
    cutoff = cutoff_ref[0]
    slot = lax.broadcasted_iota(jnp.int32, (128, 128), 0)
    lane = lax.broadcasted_iota(jnp.int32, (128, 128), 1)
    base = ((slot // 32) * 64 + (slot % 8) * 8 + (slot // 8 % 4) * 2) * COLS + lane
    for parity in range(2):
        for block in range(2):
            keep = base + (parity * COLS + block * 128) < cutoff
            parts = []
            for comp in range(2):
                rows = [
                    wave_ref[:, pl.ds(y * 8 + parity * 4 + block * 2 + comp, 8, stride=32), :]
                    for y in range(4)
                ]
                value = jnp.stack(rows, axis=1).reshape(128, 128)
                parts.append(jnp.where(keep, value, 0.0))
            masked[parity, block, 0] = parts[0]
            masked[parity, block, 1] = parts[1]
            squares[parity, block] = parts[0] * parts[0] + parts[1] * parts[1]

    for half, data_ref in enumerate((mine_ref, other_ref)):
        for zh in range(2):
            energy = jnp.zeros((128, 128), jnp.float32)
            for parity in range(2):
                for block in range(2):
                    data = [
                        data_ref[
                            :, pl.ds(zh * 12 + comp * 4 + parity * 2 + block, 8, stride=24), :
                        ].reshape(128, 128)
                        for comp in range(3)
                    ]
                    wave_re = masked[parity, block, 0]
                    wave_im = masked[parity, block, 1]
                    energy = energy + squares[parity, block] * data[2]
                    lanes = slice(block * 128, block * 128 + 128)
                    high, low = halves(data[0] * wave_re + data[1] * wave_im)
                    piece[parity, 0, 0:128, lanes] = high
                    piece[parity, 1, 0:128, lanes] = low
                    high, low = halves(data[1] * wave_re - data[0] * wave_im)
                    piece[parity, 0, 128:256, lanes] = high
                    piece[parity, 1, 128:256, lanes] = low
            scale = 1.0 / jnp.sum(energy)
            start = half == 0 and zh == 0

            def chunk_step(chunk, carry):
                begin = pl.multiple_of(chunk * 256, 256)
                both = []
                for parity in range(2):
                    table = first_ref[parity, 0, pl.ds(begin, 256), :]
                    small = first_ref[parity, 1, pl.ds(begin, 256), :]
                    both.append(
                        dot(table, piece[parity, 0])
                        + dot(small, piece[parity, 0])
                        + dot(table, piece[parity, 1])
                    )
                for wrap in range(2):
                    section = both[0] - both[1] if wrap else both[0] + both[1]
                    section_re = section[0:128]
                    section_im = section[128:256]
                    place = pl.multiple_of(wrap * 256 + chunk * 128, 128)
                    cos = turn_ref[0, pl.ds(place, 128), :]
                    sin = turn_ref[1, pl.ds(place, 128), :]
                    twist_re = section_re * cos - section_im * sin
                    twist_im = section_re * sin + section_im * cos
                    for parity in range(2):
                        if parity:
                            fold_re = twist_re[:, :128] - twist_re[:, 128:]
                            fold_im = twist_im[:, :128] - twist_im[:, 128:]
                        else:
                            fold_re = twist_re[:, :128] + twist_re[:, 128:]
                            fold_im = twist_im[:, :128] + twist_im[:, 128:]
                        high, low = halves(jnp.concatenate([fold_re, fold_im], axis=1))
                        table = last_ref[parity, 0]
                        small = last_ref[parity, 1]
                        out = dot(high, table) + dot(high, small) + dot(low, table)
                        out_re = out[:, :128]
                        out_im = out[:, 128:]
                        power = (out_re * out_re + out_im * out_im) * scale
                        if not start:
                            power = power + total[parity, pl.ds(place, 128), :]
                        total[parity, pl.ds(place, 128), :] = power
                return carry

            lax.fori_loop(0, 2, chunk_step, 0)

    for parity in range(2):
        for block in range(4):
            value = total[parity, block * 128 : block * 128 + 128, :].T
            value = value.reshape(4, 4, 8, 128)
            for y in range(4):
                network_ref[:, pl.ds(y * 8 + parity * 4 + block, 8, stride=32), :] = value[:, y]
                loud_ref[:, y, parity, pl.ds(block, 8, stride=4), :] = value[:, y]


def shards(strain, inverse_noise, slides, templates, cutoffs):
    first, turn, last = tables()
    bank = (lax.axis_index("x") * 8 + lax.axis_index("zl")) * 4 + lax.axis_index("y")
    bins = (bank * 2 + jnp.arange(2, dtype=jnp.int32)[:, None]) * COLS + jnp.arange(
        COLS, dtype=jnp.int32
    )[None, :]
    angle = ((bins * slides[0]) & (SERIES - 1)).astype(jnp.float32) * (2.0 * np.pi / SERIES)
    cos, sin = jnp.cos(angle), jnp.sin(angle)
    noise = inverse_noise[0]
    data_re = strain[0, :, 0, :]
    data_im = strain[0, :, 1, :]
    shard = jnp.stack(
        [(data_re * cos - data_im * sin) * noise, (data_re * sin + data_im * cos) * noise, noise]
    ).reshape(3, 4, 128)
    pile = lax.all_to_all(jnp.broadcast_to(shard[None], (16, 3, 4, 128)), PILE, 0, 0)
    pile = pile.reshape(192, 128)
    mine = lax.all_to_all(jnp.broadcast_to(pile[None], (16, 192, 128)), PLANE, 0, 0)
    other = lax.ppermute(mine, "core", [(0, 1), (1, 0)])
    waves = templates.reshape(ROWS, 2, 2, 128).transpose(0, 2, 1, 3).reshape(4, 256, 128)
    vmem = pl.BlockSpec(memory_space=pltpu.VMEM)
    network, loud = pl.pallas_call(
        kernel,
        out_shape=(
            jax.ShapeDtypeStruct((4, 256, 128), jnp.float32),
            jax.ShapeDtypeStruct((4, 4, 2, 32, 128), jnp.float32),
        ),
        in_specs=[pl.BlockSpec(memory_space=pltpu.SMEM)] + [vmem] * 6,
        out_specs=(vmem, vmem),
        scratch_shapes=[
            pltpu.VMEM((2, 2, 2, 128, 128), jnp.float32),
            pltpu.VMEM((2, 2, 128, 128), jnp.float32),
            pltpu.VMEM((2, 2, 256, 256), jnp.bfloat16),
            pltpu.VMEM((2, 512, 128), jnp.float32),
        ],
        compiler_params=pltpu.CompilerParams(vmem_limit_bytes=32 * 1024 * 1024),
        cost_estimate=pl.CostEstimate(
            flops=3 * 2 * 537 * 10**6, bytes_accessed=8 * 2**20, transcendentals=0
        ),
    )(cutoffs, waves, mine, other, first, turn, last)
    swapped = lax.all_to_all(loud.reshape(32, 32, 128), CHIP, 0, 0)
    peak = jnp.max(swapped, axis=0).reshape(8, 1, 4, 128)
    peak = jnp.broadcast_to(peak, (8, 4, 4, 128)).reshape(32, 4, 128)
    peaks = lax.all_to_all(peak, STACK, 0, 0)
    loudest = jnp.max(peaks.reshape(16, 2, 4, 128), axis=0).reshape(1024)
    return (loudest, network.reshape(1, SERIES))


def solution(mesh):
    fine = Mesh(mesh.devices.reshape(4, 8, 4, 2, 2), ("x", "zl", "y", "zh", "core"))
    bank = ("x", "zl", "y")
    det = ("zh", "core")
    return jax.shard_map(
        shards,
        mesh=fine,
        in_specs=(
            P(det, bank, None, None),
            P(det, bank, None),
            P(det),
            P(bank + det, None, None, None),
            P(bank + det),
        ),
        out_specs=(P(bank), P(bank + det, None)),
        check_vma=False,
    )
```

time: 1660 us -> 111 us (0.07)
  blocking collectives: 1080 us -> 87.9 us
  waiting for transfers between devices: 475 us -> 2.37 us
  matrix products: 38.6 us -> 0 us
  other arithmetic: 23 us -> 1.48 us
  local copies, waits for them, and re-layouts: 19.9 us -> 1.69 us
    all_gather x2 -> x0, blocking collectives: 962 us -> none  [the longest x1 495 us: shards(): lax.all_gather(strain, 'bank', axis=1, tiled=True)]
    pmax x1 -> x0, waiting for transfers between devices: 449 us -> none  [shards(): whole = lax.pmax(peak, ('bank', 'det'))]
    unnamed x1 -> x0, blocking collectives: 119 us -> none
    all_to_all x0 -> x4, blocking collectives: none -> 87.9 us  [the longest x1 28.2 us: shards(): lax.all_to_all(jnp.broadcast_to(shard[None], (16, 3, 4, 128)), PILE, 0, 0)]
    dot_general x8 -> x0, matrix products: 38.6 us -> none  [contract(): return jnp.einsum(form, left, right, precision=highest)]
    all_gather x2 -> x0, waiting for transfers between devices: 25.3 us -> none  [the longest x1 25.3 us: shards(): lax.all_gather(row_noise, 'det', axis=0, tiled=True)]
  transfers between devices with their start and end apart: 3 -> 1, of which waited for: 2 -> 1; matrix products, arithmetic and copies ran while one was open for 1% -> 0% of each run, Pallas kernels for 0% -> 0%
where the time goes in v1:
time: 111 us; the launch traced here: 110 us
  blocking collectives  87.9 us (79%)
  Pallas kernels  9.42 us (8%)
  starting transfers between devices  5.35 us (5%)
  waiting for transfers between devices  2.37 us (2%)
  between operations  2.01 us (2%)
  local copies, waits for them, and re-layouts  1.69 us (2%)
  other arithmetic  1.48 us (1%)
    all_to_all x1, blocking collectives, shards(): lax.all_to_all(jnp.broadcast_to(shard[None], (16, 3, 4, 128)), PILE, 0, 0)  28.2 us
    all_to_all x1, blocking collectives, shards(): lax.all_to_all(jnp.broadcast_to(pile[None], (16, 192, 128)), PLANE, 0, 0)  27 us
    all_to_all x1, blocking collectives, shards(): peaks = lax.all_to_all(peak, STACK, 0, 0)  17.2 us
    all_to_all x1, blocking collectives, shards(): swapped = lax.all_to_all(loud.reshape(32, 32, 128), CHIP, 0, 0)  15.4 us
    pallas_call x1, Pallas kernels, shards(): pl.pallas_call(kernel, out_shape=(jax.ShapeDtypeStruct((4, 256, 128), jnp...  9.42 us
    ppermute x1, starting transfers between devices, shards(): other = lax.ppermute(mine, 'core', [(0, 1), (1, 0)])  5.35 us
    ppermute x1, waiting for transfers between devices, shards(): other = lax.ppermute(mine, 'core', [(0, 1), (1, 0)])  2.37 us
  transfers between devices with their start and end apart: 1, of which 1 were waited for; matrix products, arithmetic and copies ran while one was open for 0% of the time, Pallas kernels for 0%

profile of v1, /device:TPU:1, one launch (start us, length us, event | category | flops | bytes accessed | tf_op | source)
XLA Modules:
  0.0 110.2 jit_solution(2245502233054477772)
XLA Ops:
  1.3 0.7 stack.13
  2.0 0.8 fusion.2
  2.8 0.8 subtract_multiply_fusion
  3.6 28.2 %all_to_all.20 = f32[16,3,4,128]{3,2,1,0:T(4,128)S(1)} all-to-all(f32[16,3,4,128]{3,2,1,0:T(4,128)S(1)} %broadcast_in_dim.24), channel_id=1, replica_groups=mesh['x'=4,'zl'=8,'y'=4,'zh'=2,'core'=2] {'zl','zh'}, dimensions={0} | all-to-all | bytes 196608 | tf_op jit(solution)/shard_map/all_to_all | solution.py:187
  31.8 0.1 broadcast_in_dim.26
  32.0 0.0 copy-start
  32.0 0.0 copy-start.1
  32.0 0.0 copy-start.2
  32.0 0.0 copy-start.3
  32.0 27.0 %all_to_all.21.mine_ref = f32[16,192,128]{2,1,0:T(8,128)S(1)} all-to-all(f32[16,192,128]{2,1,0:T(8,128)S(1)} %broadcast_in_dim.26), channel_id=1, replica_groups=mesh['x'=4,'zl'=8,'y'=4,'zh'=2,'core'=2] {'x','y'}, dimensions={0} | all-to-all | bytes 3145728 | tf_op jit(solution)/shard_map/all_to_all | solution.py:189
  59.0 5.4 %collective-permute-start = (f32[16,192,128]{2,1,0:T(8,128)S(1)}, f32[16,192,128]{2,1,0:T(8,128)S(1)}, u32[]{:S(2)}, u32[]{:S(2)}) collective-permute-start(f32[16,192,128]{2,1,0:T(8,128)S(1)} %all_to_all.21.mine_ref), channel_id=1, source_target_pairs={{0,1},{1,0},{2,3},{3,2},{4,5},{5,4},{6,7},{7,6},{8,9},{9,8},{10,11... | collective-permute-start | bytes 4718600 | tf_op jit(solution)/shard_map/ppermute | solution.py:190
  65.1 2.4 %collective-permute-done.other_ref = f32[16,192,128]{2,1,0:T(8,128)S(1)} collective-permute-done((f32[16,192,128]{2,1,0:T(8,128)S(1)}, f32[16,192,128]{2,1,0:T(8,128)S(1)}, u32[]{:S(2)}, u32[]{:S(2)}) %collective-permute-start) | collective-permute-done | bytes 1572896 | tf_op jit(solution)/shard_map/ppermute | solution.py:190
  67.4 0.0 copy-done
  67.4 0.0 copy-done.1
  67.4 0.0 copy-done.2
  67.4 0.0 copy-done.3
  67.4 9.4 %shard_map.95 = (f32[4,256,128]{2,1,0:T(8,128)}, f32[4,4,2,32,128]{4,3,2,1,0:T(8,128)S(1)}) custom-call(s32[1]{0:T(128)S(6)} %copy.46.cutoff_ref, f32[4,256,128]{2,1,0:T(8,128)S(1)} %bitcast.29, f32[16,192,128]{2,1,0:T(8,128)S(1)} %all_to_all.21.mine_ref, f32[16,192,128]{2,1,0:T(8,128)S(1)} %collective-permute-done.other_ref, ...), custom_call_target="tpu_custom_call" | custom-call | flops 3222000128 | bytes 8388608 | tf_op jit(solution)/shard_map/pallas_call | solution.py:193
  76.9 15.4 %all_to_all.22 = f32[32,32,128]{2,1,0:T(8,128)S(1)} all-to-all(f32[32,32,128]{2,1,0:T(8,128)S(1)} %bitcast.28), channel_id=1, replica_groups=mesh['x'=4,'zl'=8,'y'=4,'zh'=2,'core'=2] {'x','y','core'}, dimensions={0} | all-to-all | bytes 1048576 | tf_op jit(solution)/shard_map/all_to_all | solution.py:212
  92.3 17.2 %all_to_all.23 = f32[32,4,128]{2,1,0:T(4,128)S(1)} all-to-all(f32[32,4,128]{2,1,0:T(4,128)S(1)} %bitcast.31), channel_id=1, replica_groups=mesh['x'=4,'zl'=8,'y'=4,'zh'=2,'core'=2] {'zl','zh','core'}, dimensions={0} | all-to-all | bytes 131072 | tf_op jit(solution)/shard_map/all_to_all | solution.py:215
  109.6 0.6 reduce_max.19
  (7 shorter events, 0.1 us)
Async XLA Ops:
  32.0 35.5 %copy-start = (f32[1,256,2,256]{3,2,1,0:T(2,128)S(1)}, f32[1,256,2,256]{3,2,1,0:T(2,128)}, u32[]{:S(2)}) copy-start(f32[1,256,2,256]{3,2,1,0:T(2,128)} %param.11) | copy-start | bytes 1572868
  32.0 35.5 %copy-start.1 = (f32[2,512,256]{2,1,0:T(8,128)S(1)}, f32[2,512,256]{2,1,0:T(8,128)}, u32[]{:S(2)}) copy-start(f32[2,512,256]{2,1,0:T(8,128)} %constant.35.clone.turn_ref) | copy-start | bytes 3145732
  32.0 35.5 %copy-start.2 = (bf16[2,2,512,256]{3,2,1,0:T(8,128)(2,1)S(1)}, bf16[2,2,512,256]{3,2,1,0:T(8,128)(2,1)}, u32[]{:S(2)}) copy-start(bf16[2,2,512,256]{3,2,1,0:T(8,128)(2,1)} %constant.34.clone.first_ref) | copy-start | bytes 3145732
  32.0 35.4 %copy-start.3 = (bf16[2,2,256,256]{3,2,1,0:T(8,128)(2,1)S(1)}, bf16[2,2,256,256]{3,2,1,0:T(8,128)(2,1)}, u32[]{:S(2)}) copy-start(bf16[2,2,256,256]{3,2,1,0:T(8,128)(2,1)} %constant.36.clone.last_ref) | copy-start | bytes 1572868
  59.0 8.4 %collective-permute-start = (f32[16,192,128]{2,1,0:T(8,128)S(1)}, f32[16,192,128]{2,1,0:T(8,128)S(1)}, u32[]{:S(2)}, u32[]{:S(2)}) collective-permute-start(f32[16,192,128]{2,1,0:T(8,128)S(1)} %all_to_all.21.mine_ref), channel_id=1, source_target_pairs={{0,1},{1,0},{2,3},{3,2},{4,5},{5,4},{6,7},{7,6},{8,9},{9,8},{10,11... | collective-permute-start | bytes 4718600 | tf_op jit(solution)/shard_map/ppermute | solution.py:190

commit v2 on v1

v2 whole, which is shorter than its diff:
```python
import jax
import jax.numpy as jnp
import ml_dtypes
import numpy as np
from jax import lax
from jax.experimental import pallas as pl
from jax.experimental.pallas import tpu as pltpu
from jax.sharding import Mesh, PartitionSpec as P

ROWS = 256
COLS = 256
SPAN = 512
SERIES = 131072
PLANE = ("x", "y")
PILE = ("zl", "zh")
CHIP = ("x", "y", "core")
STACK = ("zl", "zh", "core")


def split(values):
    high = values.astype(ml_dtypes.bfloat16)
    low = (values - high.astype(np.float64)).astype(ml_dtypes.bfloat16)
    return np.stack([high, low])


def plane_order():
    slot = np.arange(128)
    return slot // 32, slot // 8 % 4, slot % 8


def tables():
    x, y, zl = plane_order()
    first = []
    for parity in range(2):
        row = x * 64 + zl * 8 + y * 2 + parity
        angle = 2.0 * np.pi * (np.arange(256)[:, None] * row[None, :] % SPAN) / SPAN
        cos, sin = np.cos(angle), np.sin(angle)
        whole = []
        for chunk in range(2):
            part = slice(chunk * 128, chunk * 128 + 128)
            whole.append(np.block([[cos[part], -sin[part]], [sin[part], cos[part]]]))
        first.append(split(np.concatenate(whole)))
    first = np.stack(first)
    angle = 2.0 * np.pi * (np.arange(SPAN)[:, None] * np.arange(COLS)[None, :]) / SERIES
    turn = np.stack([np.cos(angle), np.sin(angle)]).astype(np.float32)
    last = []
    for parity in range(2):
        m = 2 * (x * 32 + zl * 4 + y) + parity
        angle = 2.0 * np.pi * (np.arange(128)[:, None] * m[None, :] % COLS) / COLS
        cos, sin = np.cos(angle), np.sin(angle)
        last.append(split(np.block([[cos, sin], [-sin, cos]])))
    return first, turn, np.stack(last)


def dot(left, right):
    return jnp.dot(left, right, preferred_element_type=jnp.float32)


def halves(value):
    high = value.astype(jnp.bfloat16)
    low = (value - high.astype(jnp.float32)).astype(jnp.bfloat16)
    return high, low


def prepare(slide_ref, strain_ref, noise_ref, out_ref):
    bank = (lax.axis_index("x") * 8 + lax.axis_index("zl")) * 4 + lax.axis_index("y")
    slot = lax.broadcasted_iota(jnp.int32, (4, 128), 0)
    lane = lax.broadcasted_iota(jnp.int32, (4, 128), 1)
    bins = bank * (2 * COLS) + slot * 128 + lane
    angle = ((bins * slide_ref[0]) & (SERIES - 1)).astype(jnp.float32) * (2.0 * np.pi / SERIES)
    cos, sin = jnp.cos(angle), jnp.sin(angle)
    data_re = strain_ref[pl.ds(0, 4, stride=2), :]
    data_im = strain_ref[pl.ds(1, 4, stride=2), :]
    noise = jnp.concatenate([noise_ref[i : i + 1, :] for i in (0, 2, 1, 3)])
    turned_re = (data_re * cos - data_im * sin) * noise
    turned_im = (data_re * sin + data_im * cos) * noise
    for peer in range(16):
        out_ref[peer, 0] = turned_re
        out_ref[peer, 1] = turned_im
        out_ref[peer, 2] = noise


def mask_waves(cutoff, wave_ref, masked):
    slot = lax.broadcasted_iota(jnp.int32, (128, 128), 0)
    lane = lax.broadcasted_iota(jnp.int32, (128, 128), 1)
    base = ((slot // 32) * 64 + (slot % 8) * 8 + (slot // 8 % 4) * 2) * COLS + lane
    for parity in range(2):
        for block in range(2):
            keep = base + (parity * COLS + block * 128) < cutoff
            for comp in range(2):
                rows = [
                    wave_ref[:, pl.ds(y * 8 + parity * 4 + block * 2 + comp, 8, stride=32), :]
                    for y in range(4)
                ]
                value = jnp.stack(rows, axis=1).reshape(128, 128)
                masked[parity, block, comp] = jnp.where(keep, value, 0.0)


def product(data_ref, zh, masked, piece):
    energy = jnp.zeros((128, 128), jnp.float32)
    for parity in range(2):
        for block in range(2):
            data = [
                data_ref[
                    :, pl.ds(zh * 12 + comp * 4 + parity * 2 + block, 8, stride=24), :
                ].reshape(128, 128)
                for comp in range(3)
            ]
            wave_re = masked[parity, block, 0]
            wave_im = masked[parity, block, 1]
            energy = energy + (wave_re * wave_re + wave_im * wave_im) * data[2]
            lanes = slice(block * 128, block * 128 + 128)
            high, low = halves(data[0] * wave_re + data[1] * wave_im)
            piece[zh, parity, 0, 0:128, lanes] = high
            piece[zh, parity, 1, 0:128, lanes] = low
            high, low = halves(data[1] * wave_re - data[0] * wave_im)
            piece[zh, parity, 0, 128:256, lanes] = high
            piece[zh, parity, 1, 128:256, lanes] = low
    return 1.0 / jnp.sum(energy)


def first_stage(zh, chunk, first_ref, piece):
    both = []
    for parity in range(2):
        table = first_ref[parity, 0, chunk * 256 : chunk * 256 + 256, :]
        small = first_ref[parity, 1, chunk * 256 : chunk * 256 + 256, :]
        both.append(
            dot(table, piece[zh, parity, 0])
            + dot(small, piece[zh, parity, 0])
            + dot(table, piece[zh, parity, 1])
        )
    return both


def last_stage(chunk, both, scale, turn_ref, last_ref, add):
    for wrap in range(2):
        section = both[0] - both[1] if wrap else both[0] + both[1]
        section_re = section[0:128]
        section_im = section[128:256]
        place = wrap * 256 + chunk * 128
        cos = turn_ref[0, place : place + 128, :]
        sin = turn_ref[1, place : place + 128, :]
        twist_re = section_re * cos - section_im * sin
        twist_im = section_re * sin + section_im * cos
        for parity in range(2):
            if parity:
                fold_re = twist_re[:, :128] - twist_re[:, 128:]
                fold_im = twist_im[:, :128] - twist_im[:, 128:]
            else:
                fold_re = twist_re[:, :128] + twist_re[:, 128:]
                fold_im = twist_im[:, :128] + twist_im[:, 128:]
            high, low = halves(jnp.concatenate([fold_re, fold_im], axis=1))
            table = last_ref[parity, 0]
            small = last_ref[parity, 1]
            out = dot(high, table) + dot(high, small) + dot(low, table)
            out_re = out[:, :128]
            out_im = out[:, 128:]
            add(parity, place, (out_re * out_re + out_im * out_im) * scale)


def pipeline(data_ref, masked, first_ref, turn_ref, last_ref, piece, add):
    steps = [(zh, chunk) for zh in range(2) for chunk in range(2)]
    scales = [product(data_ref, 0, masked, piece)]
    held = first_stage(0, 0, first_ref, piece)
    for step, (zh, chunk) in enumerate(steps):
        if step == 0:
            scales.append(product(data_ref, 1, masked, piece))
        after = first_stage(*steps[step + 1], first_ref, piece) if step < 3 else None
        last_stage(chunk, held, scales[zh], turn_ref, last_ref, add[zh])
        held = after


def own_kernel(cutoff_ref, wave_ref, data_ref, first_ref, turn_ref, last_ref, total, masked, piece):
    mask_waves(cutoff_ref[0], wave_ref, masked)

    def begin(parity, place, power):
        total[parity, place : place + 128, :] = power

    def more(parity, place, power):
        total[parity, place : place + 128, :] += power

    pipeline(data_ref, masked, first_ref, turn_ref, last_ref, piece, (begin, more))


def rest_kernel(
    masked, carry_ref, data_ref, first_ref, turn_ref, last_ref, network_ref, loud_ref, total, piece
):
    def more(parity, place, power):
        total[parity, place : place + 128, :] = carry_ref[parity, place : place + 128, :] + power

    def close(parity, place, power):
        block = place // 128
        value = (total[parity, place : place + 128, :] + power).T.reshape(4, 4, 8, 128)
        for y in range(4):
            network_ref[:, pl.ds(y * 8 + parity * 4 + block, 8, stride=32), :] = value[:, y]
            loud_ref[:, y, parity, pl.ds(block, 8, stride=4), :] = value[:, y]

    pipeline(data_ref, masked, first_ref, turn_ref, last_ref, piece, (more, close))


def shards(strain, inverse_noise, slides, templates, cutoffs):
    first, turn, last = tables()
    smem = pl.BlockSpec(memory_space=pltpu.SMEM)
    vmem = pl.BlockSpec(memory_space=pltpu.VMEM)
    params = pltpu.CompilerParams(vmem_limit_bytes=32 * 1024 * 1024)
    cost = pl.CostEstimate(flops=3 * 537 * 10**6, bytes_accessed=6 * 2**20, transcendentals=0)
    shard = pl.pallas_call(
        prepare,
        out_shape=jax.ShapeDtypeStruct((16, 3, 4, 128), jnp.float32),
        in_specs=[smem, vmem, vmem],
        out_specs=vmem,
    )(
        slides,
        strain.reshape(2, 2, 2, 128).transpose(0, 2, 1, 3).reshape(8, 128),
        inverse_noise.reshape(2, 2, 128).transpose(1, 0, 2).reshape(4, 128),
    )
    pile = lax.all_to_all(shard, PILE, 0, 0).reshape(192, 128)
    mine = lax.all_to_all(jnp.broadcast_to(pile[None], (16, 192, 128)), PLANE, 0, 0)
    other = lax.ppermute(mine, "core", [(0, 1), (1, 0)])
    waves = templates.reshape(ROWS, 2, 2, 128).transpose(0, 2, 1, 3).reshape(4, 256, 128)
    carry, masked = pl.pallas_call(
        own_kernel,
        out_shape=(
            jax.ShapeDtypeStruct((2, 512, 128), jnp.float32),
            jax.ShapeDtypeStruct((2, 2, 2, 128, 128), jnp.float32),
        ),
        in_specs=[smem] + [vmem] * 5,
        out_specs=(vmem, vmem),
        scratch_shapes=[pltpu.VMEM((2, 2, 2, 256, 256), jnp.bfloat16)],
        compiler_params=params,
        cost_estimate=cost,
    )(cutoffs, waves, mine, first, turn, last)
    network, loud = pl.pallas_call(
        rest_kernel,
        out_shape=(
            jax.ShapeDtypeStruct((4, 256, 128), jnp.float32),
            jax.ShapeDtypeStruct((4, 4, 2, 32, 128), jnp.float32),
        ),
        in_specs=[vmem] * 6,
        out_specs=(vmem, vmem),
        scratch_shapes=[
            pltpu.VMEM((2, 512, 128), jnp.float32),
            pltpu.VMEM((2, 2, 2, 256, 256), jnp.bfloat16),
        ],
        compiler_params=params,
        cost_estimate=cost,
    )(masked, carry, other, first, turn, last)
    swapped = lax.all_to_all(loud.reshape(32, 32, 128), CHIP, 0, 0)
    peak = jnp.max(swapped, axis=0).reshape(8, 1, 4, 128)
    peak = jnp.broadcast_to(peak, (8, 4, 4, 128)).reshape(32, 4, 128)
    peaks = lax.all_to_all(peak, STACK, 0, 0)
    loudest = jnp.max(peaks.reshape(16, 2, 4, 128), axis=0).reshape(1024)
    return (loudest, network.reshape(1, SERIES))


def solution(mesh):
    fine = Mesh(mesh.devices.reshape(4, 8, 4, 2, 2), ("x", "zl", "y", "zh", "core"))
    bank = ("x", "zl", "y")
    det = ("zh", "core")
    return jax.shard_map(
        shards,
        mesh=fine,
        in_specs=(
            P(det, bank, None, None),
            P(det, bank, None),
            P(det),
            P(bank + det, None, None, None),
            P(bank + det),
        ),
        out_specs=(P(bank), P(bank + det, None)),
        check_vma=False,
    )
```

time: 111 us -> 104 us (0.937)
  waiting for transfers between devices: 2.37 us -> 0.01 us
  Pallas kernels: 9.42 us -> 7.9 us
  local copies, waits for them, and re-layouts: 1.69 us -> 0.18 us
    ppermute x1, waiting for transfers between devices: 2.37 us -> 0.01 us  [shards(): other = lax.ppermute(mine, 'core', [(0, 1), (1, 0)])]
    pallas_call x1 -> x3, Pallas kernels: 9.42 us -> 7.9 us  [the longest x1 3.67 us: shards(): pl.pallas_call(rest_kernel, out_shape=(jax.ShapeDtypeStruct((4, 256, 128)...]
  transfers between devices with their start and end apart: 1 -> 1, of which waited for: 1 -> 0; matrix products, arithmetic and copies ran while one was open for 0% -> 0% of each run, Pallas kernels for 0% -> 3%
where the time goes in v2:
time: 104 us
  blocking collectives  87.9 us (85%)
  Pallas kernels  7.9 us (8%)
  starting transfers between devices  5.35 us (5%)
  between operations  2.03 us (2%)
    all_to_all x1, blocking collectives, shards(): pile = lax.all_to_all(shard, PILE, 0, 0).reshape(192, 128)  28.4 us
    all_to_all x1, blocking collectives, shards(): lax.all_to_all(jnp.broadcast_to(pile[None], (16, 192, 128)), PLANE, 0, 0)  27 us
    all_to_all x1, blocking collectives, shards(): peaks = lax.all_to_all(peak, STACK, 0, 0)  17.3 us
    all_to_all x1, blocking collectives, shards(): swapped = lax.all_to_all(loud.reshape(32, 32, 128), CHIP, 0, 0)  15.1 us
    ppermute x1, starting transfers between devices, shards(): other = lax.ppermute(mine, 'core', [(0, 1), (1, 0)])  5.35 us
    pallas_call x1, Pallas kernels, shards(): pl.pallas_call(rest_kernel, out_shape=(jax.ShapeDtypeStruct((4, 256, 128)...  3.67 us
    pallas_call x1, Pallas kernels, shards(): pl.pallas_call(own_kernel, out_shape=(jax.ShapeDtypeStruct((2, 512, 128),...  2.83 us
  transfers between devices with their start and end apart: 1, of which 0 were waited for; matrix products, arithmetic and copies ran while one was open for 0% of the time, Pallas kernels for 3%

profile of v2, /device:TPU:1, one launch (start us, length us, event | category | flops | bytes accessed | tf_op | source)
XLA Modules:
  0.0 104.0 jit_solution(17433430756187824880)
XLA Ops:
  1.3 1.4 %shard_map.95 = f32[16,3,4,128]{3,2,1,0:T(4,128)} custom-call(s32[1]{0:T(128)S(6)} %copy.33.slide_ref, f32[8,128]{1,0:T(8,128)} %bitcast.28, f32[4,128]{1,0:T(4,128)} %bitcast.30), custom_call_target="tpu_custom_call" | custom-call | tf_op jit(solution)/shard_map/pallas_call | solution.py:207
  2.7 28.4 %all_to_all.20 = f32[16,3,4,128]{3,2,1,0:T(4,128)S(1)} all-to-all(f32[16,3,4,128]{3,2,1,0:T(4,128)} %shard_map.95), channel_id=1, replica_groups=mesh['x'=4,'zl'=8,'y'=4,'zh'=2,'core'=2] {'zl','zh'}, dimensions={0} | all-to-all | bytes 196608 | tf_op jit(solution)/shard_map/all_to_all | solution.py:217
  31.1 0.1 broadcast_in_dim.15
  31.2 0.0 copy-start
  31.2 0.0 copy-start.1
  31.2 0.0 copy-start.2
  31.2 0.0 copy-start.3
  31.3 27.0 %all_to_all.21.data_ref = f32[16,192,128]{2,1,0:T(8,128)S(1)} all-to-all(f32[16,192,128]{2,1,0:T(8,128)S(1)} %broadcast_in_dim.15), channel_id=1, replica_groups=mesh['x'=4,'zl'=8,'y'=4,'zh'=2,'core'=2] {'x','y'}, dimensions={0} | all-to-all | bytes 3145728 | tf_op jit(solution)/shard_map/all_to_all | solution.py:218
  58.3 5.4 %collective-permute-start = (f32[16,192,128]{2,1,0:T(8,128)S(1)}, f32[16,192,128]{2,1,0:T(8,128)S(1)}, u32[]{:S(2)}, u32[]{:S(2)}) collective-permute-start(f32[16,192,128]{2,1,0:T(8,128)S(1)} %all_to_all.21.data_ref), channel_id=1, source_target_pairs={{0,1},{1,0},{2,3},{3,2},{4,5},{5,4},{6,7},{7,6},{8,9},{9,8},{10,11... | collective-permute-start | bytes 4718600 | tf_op jit(solution)/shard_map/ppermute | solution.py:219
  64.3 0.0 copy-done
  64.3 0.0 copy-done.1
  64.3 0.0 copy-done.2
  64.3 0.0 copy-done.3
  64.3 2.8 %shard_map.96 = (f32[2,512,128]{2,1,0:T(8,128)S(1)}, f32[2,2,2,128,128]{4,3,2,1,0:T(8,128)S(1)}) custom-call(s32[1]{0:T(128)S(6)} %copy.34.cutoff_ref, f32[4,256,128]{2,1,0:T(8,128)S(1)} %bitcast.23, f32[16,192,128]{2,1,0:T(8,128)S(1)} %all_to_all.21.data_ref, bf16[2,2,512,256]{3,2,1,0:T(8,128)(2,1)S(1)} %copy-done.2, f32[2,512,256]{2,1,0:T(8,128)S(1)} %copy-done.1, ...), custom_call_target="tpu_custom_call" | custom-call | flops 1611000064 | bytes 6291456 | tf_op jit(solution)/shard_map/pallas_call | solution.py:221
  67.2 0.0 collective-permute-done.data_ref
  67.2 3.7 %shard_map.97 = (f32[4,256,128]{2,1,0:T(8,128)}, f32[4,4,2,32,128]{4,3,2,1,0:T(8,128)S(1)}) custom-call(f32[2,2,2,128,128]{4,3,2,1,0:T(8,128)S(1)} %get-tuple-element.6.masked, f32[2,512,128]{2,1,0:T(8,128)S(1)} %get-tuple-element.7.carry_ref, f32[16,192,128]{2,1,0:T(8,128)S(1)} %collective-permute-done.data_ref, bf16[2,2,512,256]{3,2,1,0:T(8,128)(2,1)S(1)} %copy-done.2, ...), custom_call_target="tpu_custom_call" | custom-call | flops 1611000064 | bytes 6291456 | tf_op jit(solution)/shard_map/pallas_call | solution.py:233
  70.9 15.1 %all_to_all.22 = f32[32,32,128]{2,1,0:T(8,128)S(1)} all-to-all(f32[32,32,128]{2,1,0:T(8,128)S(1)} %bitcast.22), channel_id=1, replica_groups=mesh['x'=4,'zl'=8,'y'=4,'zh'=2,'core'=2] {'x','y','core'}, dimensions={0} | all-to-all | bytes 1048576 | tf_op jit(solution)/shard_map/all_to_all | solution.py:248
  86.1 17.3 %all_to_all.23 = f32[32,4,128]{2,1,0:T(4,128)S(1)} all-to-all(f32[32,4,128]{2,1,0:T(4,128)S(1)} %bitcast.25), channel_id=1, replica_groups=mesh['x'=4,'zl'=8,'y'=4,'zh'=2,'core'=2] {'zl','zh','core'}, dimensions={0} | all-to-all | bytes 131072 | tf_op jit(solution)/shard_map/all_to_all | solution.py:251
  103.4 0.6 reduce_max.19
  (2 shorter events, 0.1 us)
Async XLA Ops:
  31.2 33.1 %copy-start = (f32[1,256,2,256]{3,2,1,0:T(2,128)S(1)}, f32[1,256,2,256]{3,2,1,0:T(2,128)}, u32[]{:S(2)}) copy-start(f32[1,256,2,256]{3,2,1,0:T(2,128)} %param.11) | copy-start | bytes 1572868
  31.2 33.1 %copy-start.1 = (f32[2,512,256]{2,1,0:T(8,128)S(1)}, f32[2,512,256]{2,1,0:T(8,128)}, u32[]{:S(2)}) copy-start(f32[2,512,256]{2,1,0:T(8,128)} %constant.9.clone.turn_ref) | copy-start | bytes 3145732
  31.2 33.1 %copy-start.2 = (bf16[2,2,512,256]{3,2,1,0:T(8,128)(2,1)S(1)}, bf16[2,2,512,256]{3,2,1,0:T(8,128)(2,1)}, u32[]{:S(2)}) copy-start(bf16[2,2,512,256]{3,2,1,0:T(8,128)(2,1)} %constant.8.clone.first_ref) | copy-start | bytes 3145732
  31.2 33.1 %copy-start.3 = (bf16[2,2,256,256]{3,2,1,0:T(8,128)(2,1)S(1)}, bf16[2,2,256,256]{3,2,1,0:T(8,128)(2,1)}, u32[]{:S(2)}) copy-start(bf16[2,2,256,256]{3,2,1,0:T(8,128)(2,1)} %constant.10.clone.last_ref) | copy-start | bytes 1572868
  58.3 8.9 %collective-permute-start = (f32[16,192,128]{2,1,0:T(8,128)S(1)}, f32[16,192,128]{2,1,0:T(8,128)S(1)}, u32[]{:S(2)}, u32[]{:S(2)}) collective-permute-start(f32[16,192,128]{2,1,0:T(8,128)S(1)} %all_to_all.21.data_ref), channel_id=1, source_target_pairs={{0,1},{1,0},{2,3},{3,2},{4,5},{5,4},{6,7},{7,6},{8,9},{9,8},{10,11... | collective-permute-start | bytes 4718600 | tf_op jit(solution)/shard_map/ppermute | solution.py:219

commit v3 on v2

--- a/solution.py
+++ b/solution.py
@@ -11,10 +11,13 @@
 COLS = 256
 SPAN = 512
 SERIES = 131072
-PLANE = ("x", "y")
-PILE = ("zl", "zh")
-CHIP = ("x", "y", "core")
-STACK = ("zl", "zh", "core")
+AXES = ("x1", "x0", "z2", "z1", "z0", "y1", "y0", "zh", "core")
+BANK = AXES[:7]
+DET = AXES[7:]
+PLANE = ("x1", "y1", "x0", "y0")
+PILE = ("zh", "z2", "z1", "z0")
+CHIP = ("x1", "x0", "y1", "y0", "core")
+STACK = ("z2", "z1", "z0", "zh", "core")
 
 
 def split(values):
@@ -23,16 +26,17 @@
     return np.stack([high, low])
 
 
-def plane_order():
+def slot_rows(slot):
+    x = slot // 64 * 2 + slot // 16 % 2
+    y = slot // 32 % 2 * 2 + slot // 8 % 2
+    return x * 64 + slot % 8 * 8 + y * 2
+
+
+def tables():
     slot = np.arange(128)
-    return slot // 32, slot // 8 % 4, slot % 8
-
-
-def tables():
-    x, y, zl = plane_order()
     first = []
     for parity in range(2):
-        row = x * 64 + zl * 8 + y * 2 + parity
+        row = slot_rows(slot) + parity
         angle = 2.0 * np.pi * (np.arange(256)[:, None] * row[None, :] % SPAN) / SPAN
         cos, sin = np.cos(angle), np.sin(angle)
         whole = []
@@ -45,7 +49,7 @@
     turn = np.stack([np.cos(angle), np.sin(angle)]).astype(np.float32)
     last = []
     for parity in range(2):
-        m = 2 * (x * 32 + zl * 4 + y) + parity
+        m = 2 * (slot // 32 * 32 + slot % 8 * 4 + slot // 8 % 4) + parity
         angle = 2.0 * np.pi * (np.arange(128)[:, None] * m[None, :] % COLS) / COLS
         cos, sin = np.cos(angle), np.sin(angle)
         last.append(split(np.block([[cos, sin], [-sin, cos]])))
@@ -62,37 +66,52 @@
     return high, low
 
 
-def prepare(slide_ref, strain_ref, noise_ref, out_ref):
-    bank = (lax.axis_index("x") * 8 + lax.axis_index("zl")) * 4 + lax.axis_index("y")
+def prepare(
+    slides_hbm, cutoffs_hbm, strain_hbm, noise_hbm, out_ref, cut_ref, slide, cutoff, strain, noise, sems
+):
+    pairs = ((slides_hbm, slide), (cutoffs_hbm, cutoff), (strain_hbm, strain), (noise_hbm, noise))
+    copies = [pltpu.make_async_copy(a, b, sems.at[i]) for i, (a, b) in enumerate(pairs)]
+    for copy in copies:
+        copy.start()
+    bank = jnp.int32(0)
+    for name in BANK:
+        bank = bank * 2 + lax.axis_index(name)
     slot = lax.broadcasted_iota(jnp.int32, (4, 128), 0)
     lane = lax.broadcasted_iota(jnp.int32, (4, 128), 1)
     bins = bank * (2 * COLS) + slot * 128 + lane
-    angle = ((bins * slide_ref[0]) & (SERIES - 1)).astype(jnp.float32) * (2.0 * np.pi / SERIES)
+    for copy in copies:
+        copy.wait()
+    cut_ref[...] = jnp.full((8, 128), cutoff[0], jnp.int32)
+    angle = ((bins * slide[0]) & (SERIES - 1)).astype(jnp.float32) * (2.0 * np.pi / SERIES)
     cos, sin = jnp.cos(angle), jnp.sin(angle)
-    data_re = strain_ref[pl.ds(0, 4, stride=2), :]
-    data_im = strain_ref[pl.ds(1, 4, stride=2), :]
-    noise = jnp.concatenate([noise_ref[i : i + 1, :] for i in (0, 2, 1, 3)])
-    turned_re = (data_re * cos - data_im * sin) * noise
-    turned_im = (data_re * sin + data_im * cos) * noise
+    data_re = strain[pl.ds(0, 4, stride=2), :]
+    data_im = strain[pl.ds(1, 4, stride=2), :]
+    weight = jnp.concatenate([noise[i : i + 1, :] for i in (0, 2, 1, 3)])
+    turned_re = (data_re * cos - data_im * sin) * weight
+    turned_im = (data_re * sin + data_im * cos) * weight
     for peer in range(16):
         out_ref[peer, 0] = turned_re
         out_ref[peer, 1] = turned_im
-        out_ref[peer, 2] = noise
-
-
-def mask_waves(cutoff, wave_ref, masked):
+        out_ref[peer, 2] = weight
+
+
+def mask_waves(cut_ref, wave_ref, masked):
+    cutoff = cut_ref[0:1, :]
     slot = lax.broadcasted_iota(jnp.int32, (128, 128), 0)
     lane = lax.broadcasted_iota(jnp.int32, (128, 128), 1)
-    base = ((slot // 32) * 64 + (slot % 8) * 8 + (slot // 8 % 4) * 2) * COLS + lane
+    base = slot_rows(slot) * COLS + lane
     for parity in range(2):
         for block in range(2):
             keep = base + (parity * COLS + block * 128) < cutoff
             for comp in range(2):
-                rows = [
-                    wave_ref[:, pl.ds(y * 8 + parity * 4 + block * 2 + comp, 8, stride=32), :]
-                    for y in range(4)
-                ]
-                value = jnp.stack(rows, axis=1).reshape(128, 128)
+                value = jnp.concatenate(
+                    [
+                        wave_ref[slot_rows(8 * i) * 4 // 256, pl.ds(
+                            slot_rows(8 * i) * 4 % 256 + parity * 4 + block * 2 + comp, 8, stride=32
+                        ), :]
+                        for i in range(16)
+                    ]
+                )
                 masked[parity, block, comp] = jnp.where(keep, value, 0.0)
 
 
@@ -102,7 +121,7 @@
         for block in range(2):
             data = [
                 data_ref[
-                    :, pl.ds(zh * 12 + comp * 4 + parity * 2 + block, 8, stride=24), :
+                    :, pl.ds(zh * 96 + comp * 4 + parity * 2 + block, 8, stride=12), :
                 ].reshape(128, 128)
                 for comp in range(3)
             ]
@@ -170,8 +189,8 @@
         held = after
 
 
-def own_kernel(cutoff_ref, wave_ref, data_ref, first_ref, turn_ref, last_ref, total, masked, piece):
-    mask_waves(cutoff_ref[0], wave_ref, masked)
+def own_kernel(cut_ref, wave_ref, data_ref, first_ref, turn_ref, last_ref, total, masked, piece):
+    mask_waves(cut_ref, wave_ref, masked)
 
     def begin(parity, place, power):
         total[parity, place : place + 128, :] = power
@@ -200,17 +219,27 @@
 
 def shards(strain, inverse_noise, slides, templates, cutoffs):
     first, turn, last = tables()
-    smem = pl.BlockSpec(memory_space=pltpu.SMEM)
     vmem = pl.BlockSpec(memory_space=pltpu.VMEM)
     params = pltpu.CompilerParams(vmem_limit_bytes=32 * 1024 * 1024)
     cost = pl.CostEstimate(flops=3 * 537 * 10**6, bytes_accessed=6 * 2**20, transcendentals=0)
-    shard = pl.pallas_call(
+    shard, cut = pl.pallas_call(
         prepare,
-        out_shape=jax.ShapeDtypeStruct((16, 3, 4, 128), jnp.float32),
-        in_specs=[smem, vmem, vmem],
-        out_specs=vmem,
+        out_shape=(
+            jax.ShapeDtypeStruct((16, 3, 4, 128), jnp.float32),
+            jax.ShapeDtypeStruct((8, 128), jnp.int32),
+        ),
+        in_specs=[pl.BlockSpec(memory_space=pltpu.HBM)] * 4,
+        out_specs=(vmem, vmem),
+        scratch_shapes=[
+            pltpu.SMEM((1,), jnp.int32),
+            pltpu.SMEM((1,), jnp.int32),
+            pltpu.VMEM((8, 128), jnp.float32),
+            pltpu.VMEM((4, 128), jnp.float32),
+            pltpu.SemaphoreType.DMA((4,)),
+        ],
     )(
         slides,
+        cutoffs,
         strain.reshape(2, 2, 2, 128).transpose(0, 2, 1, 3).reshape(8, 128),
         inverse_noise.reshape(2, 2, 128).transpose(1, 0, 2).reshape(4, 128),
     )
@@ -224,12 +253,12 @@
             jax.ShapeDtypeStruct((2, 512, 128), jnp.float32),
             jax.ShapeDtypeStruct((2, 2, 2, 128, 128), jnp.float32),
         ),
-        in_specs=[smem] + [vmem] * 5,
+        in_specs=[vmem] * 6,
         out_specs=(vmem, vmem),
         scratch_shapes=[pltpu.VMEM((2, 2, 2, 256, 256), jnp.bfloat16)],
         compiler_params=params,
         cost_estimate=cost,
-    )(cutoffs, waves, mine, first, turn, last)
+    )(cut, waves, mine, first, turn, last)
     network, loud = pl.pallas_call(
         rest_kernel,
         out_shape=(
@@ -254,19 +283,17 @@
 
 
 def solution(mesh):
-    fine = Mesh(mesh.devices.reshape(4, 8, 4, 2, 2), ("x", "zl", "y", "zh", "core"))
-    bank = ("x", "zl", "y")
-    det = ("zh", "core")
+    fine = Mesh(mesh.devices.reshape((2,) * 9), AXES)
     return jax.shard_map(
         shards,
         mesh=fine,
         in_specs=(
-            P(det, bank, None, None),
-            P(det, bank, None),
-            P(det),
-            P(bank + det, None, None, None),
-            P(bank + det),
-        ),
-        out_specs=(P(bank), P(bank + det, None)),
+            P(DET, BANK, None, None),
+            P(DET, BANK, None),
+            P(DET),
+            P(AXES, None, None, None),
+            P(AXES),
+        ),
+        out_specs=(P(BANK), P(AXES, None)),
         check_vma=False,
     )

time: 104 us -> 105 us (level)
  transfers between devices with their start and end apart: 1 -> 1, of which waited for: 0 -> 1; matrix products, arithmetic and copies ran while one was open for 0% -> 0% of each run, Pallas kernels for 3% -> 3%
where the time goes in v3:
time: 105 us; the launch traced here: 104 us
  blocking collectives  87.8 us (84%)
  Pallas kernels  7.87 us (7%)
  starting transfers between devices  5.52 us (5%)
  between operations  2.04 us (2%)
    all_to_all x1, blocking collectives, shards(): pile = lax.all_to_all(shard, PILE, 0, 0).reshape(192, 128)  27.6 us
    all_to_all x1, blocking collectives, shards(): lax.all_to_all(jnp.broadcast_to(pile[None], (16, 192, 128)), PLANE, 0, 0)  26.7 us
    all_to_all x1, blocking collectives, shards(): peaks = lax.all_to_all(peak, STACK, 0, 0)  18.2 us
    all_to_all x1, blocking collectives, shards(): swapped = lax.all_to_all(loud.reshape(32, 32, 128), CHIP, 0, 0)  15.3 us
    ppermute x1, starting transfers between devices, shards(): other = lax.ppermute(mine, 'core', [(0, 1), (1, 0)])  5.52 us
    pallas_call x1, Pallas kernels, shards(): pl.pallas_call(rest_kernel, out_shape=(jax.ShapeDtypeStruct((4, 256, 128)...  3.61 us
    pallas_call x1, Pallas kernels, shards(): pl.pallas_call(own_kernel, out_shape=(jax.ShapeDtypeStruct((2, 512, 128),...  2.82 us
  transfers between devices with their start and end apart: 1, of which 1 were waited for; matrix products, arithmetic and copies ran while one was open for 0% of the time, Pallas kernels for 3%

profile of v3, /device:TPU:1, one launch (start us, length us, event | category | flops | bytes accessed | tf_op | source)
XLA Modules:
  0.0 104.2 jit_solution(1281145987766126730)
XLA Ops:
  1.9 1.4 %shard_map.95 = (f32[16,3,4,128]{3,2,1,0:T(4,128)}, s32[8,128]{1,0:T(8,128)}) custom-call(s32[1]{0:T(128)S(6)} %copy.33.slides_hbm, s32[1]{0:T(128)S(6)} %copy.34.cutoffs_hbm, f32[8,128]{1,0:T(8,128)} %bitcast.29, f32[4,128]{1,0:T(4,128)} %bitcast.30), custom_call_target="tpu_custom_call" | custom-call | tf_op jit(solution)/shard_map/pallas_call | solution.py:225
  3.4 27.6 %all_to_all.20 = f32[16,3,4,128]{3,2,1,0:T(4,128)S(1)} all-to-all(f32[16,3,4,128]{3,2,1,0:T(4,128)} %get-tuple-element.9), channel_id=1, replica_groups=mesh['x1'=2,'x0'=2,'z2'=2,'z1'=2,'z0'=2,'y1'=2,'y0'=2,'zh'=2,'core'=2] {..., dimensions={0} | all-to-all | bytes 196608 | tf_op jit(solution)/shard_map/all_to_all | solution.py:246
  31.0 0.0 copy-start.4
  31.0 0.1 broadcast_in_dim.15
  31.1 0.0 copy-start
  31.1 0.0 copy-start.1
  31.2 0.0 copy-start.2
  31.2 0.0 copy-start.3
  31.2 26.7 %all_to_all.21.data_ref = f32[16,192,128]{2,1,0:T(8,128)S(1)} all-to-all(f32[16,192,128]{2,1,0:T(8,128)S(1)} %broadcast_in_dim.15), channel_id=1, replica_groups=mesh['x1'=2,'x0'=2,'z2'=2,'z1'=2,'z0'=2,'y1'=2,'y0'=2,'zh'=2,'core'=2] {..., dimensions={0} | all-to-all | bytes 3145728 | tf_op jit(solution)/shard_map/all_to_all | solution.py:247
  57.9 5.5 %collective-permute-start = (f32[16,192,128]{2,1,0:T(8,128)S(1)}, f32[16,192,128]{2,1,0:T(8,128)S(1)}, u32[]{:S(2)}, u32[]{:S(2)}) collective-permute-start(f32[16,192,128]{2,1,0:T(8,128)S(1)} %all_to_all.21.data_ref), channel_id=1, source_target_pairs={{0,1},{1,0},{2,3},{3,2},{4,5},{5,4},{6,7},{7,6},{8,9},{9,8},{10,11... | collective-permute-start | bytes 4718600 | tf_op jit(solution)/shard_map/ppermute | solution.py:248
  63.5 0.0 copy-done.4
  63.5 0.0 copy-done
  63.5 0.0 copy-done.1
  63.5 0.0 copy-done.2
  63.5 0.0 copy-done.3
  63.5 2.8 %shard_map.96 = (f32[2,512,128]{2,1,0:T(8,128)S(1)}, f32[2,2,2,128,128]{4,3,2,1,0:T(8,128)S(1)}) custom-call(s32[8,128]{1,0:T(8,128)S(1)} %copy-done.1, f32[4,256,128]{2,1,0:T(8,128)S(1)} %bitcast.23, f32[16,192,128]{2,1,0:T(8,128)S(1)} %all_to_all.21.data_ref, bf16[2,2,512,256]{3,2,1,0:T(8,128)(2,1)S(1)} %copy-done.3, f32[2,512,256]{2,1,0:T(8,128)S(1)} %copy-done.2, ...), custom_call_target="tpu_custom_call" | custom-call | flops 1611000064 | bytes 6291456 | tf_op jit(solution)/shard_map/pallas_call | solution.py:250
  66.3 0.1 collective-permute-done.data_ref
  66.5 3.6 %shard_map.97 = (f32[4,256,128]{2,1,0:T(8,128)}, f32[4,4,2,32,128]{4,3,2,1,0:T(8,128)S(1)}) custom-call(f32[2,2,2,128,128]{4,3,2,1,0:T(8,128)S(1)} %get-tuple-element.10.masked, f32[2,512,128]{2,1,0:T(8,128)S(1)} %get-tuple-element.11.carry_ref, f32[16,192,128]{2,1,0:T(8,128)S(1)} %collective-permute-done.data_ref, bf16[2,2,512,256]{3,2,1,0:T(8,128)(2,1)S(1)} %copy-done.3, ...), custom_call_target="tpu_custom_call" | custom-call | flops 1611000064 | bytes 6291456 | tf_op jit(solution)/shard_map/pallas_call | solution.py:262
  70.1 15.3 %all_to_all.22 = f32[32,32,128]{2,1,0:T(8,128)S(1)} all-to-all(f32[32,32,128]{2,1,0:T(8,128)S(1)} %bitcast.22), channel_id=1, replica_groups=mesh['x1'=2,'x0'=2,'z2'=2,'z1'=2,'z0'=2,'y1'=2,'y0'=2,'zh'=2,'core'=2] {..., dimensions={0} | all-to-all | bytes 1048576 | tf_op jit(solution)/shard_map/all_to_all | solution.py:277
  85.4 18.2 %all_to_all.23 = f32[32,4,128]{2,1,0:T(4,128)S(1)} all-to-all(f32[32,4,128]{2,1,0:T(4,128)S(1)} %bitcast.25), channel_id=1, replica_groups=mesh['x1'=2,'x0'=2,'z2'=2,'z1'=2,'z0'=2,'y1'=2,'y0'=2,'zh'=2,'core'=2] {..., dimensions={0} | all-to-all | bytes 131072 | tf_op jit(solution)/shard_map/all_to_all | solution.py:280
  103.6 0.6 reduce_max.19
  (2 shorter events, 0.1 us)
Async XLA Ops:
  31.0 32.5 %copy-start.4 = (bf16[2,2,256,256]{3,2,1,0:T(8,128)(2,1)S(1)}, bf16[2,2,256,256]{3,2,1,0:T(8,128)(2,1)}, u32[]{:S(2)}) copy-start(bf16[2,2,256,256]{3,2,1,0:T(8,128)(2,1)} %constant.10.clone.last_ref) | copy-start | bytes 1572868
  31.1 32.3 %copy-start = (f32[1,256,2,256]{3,2,1,0:T(2,128)S(1)}, f32[1,256,2,256]{3,2,1,0:T(2,128)}, u32[]{:S(2)}) copy-start(f32[1,256,2,256]{3,2,1,0:T(2,128)} %param.11) | copy-start | bytes 1572868
  31.1 32.3 %copy-start.1 = (s32[8,128]{1,0:T(8,128)S(1)}, s32[8,128]{1,0:T(8,128)}, u32[]{:S(2)}) copy-start(s32[8,128]{1,0:T(8,128)} %get-tuple-element.8.cut_ref) | copy-start | bytes 12292
  31.2 32.3 %copy-start.2 = (f32[2,512,256]{2,1,0:T(8,128)S(1)}, f32[2,512,256]{2,1,0:T(8,128)}, u32[]{:S(2)}) copy-start(f32[2,512,256]{2,1,0:T(8,128)} %constant.9.clone.turn_ref) | copy-start | bytes 3145732
  31.2 32.3 %copy-start.3 = (bf16[2,2,512,256]{3,2,1,0:T(8,128)(2,1)S(1)}, bf16[2,2,512,256]{3,2,1,0:T(8,128)(2,1)}, u32[]{:S(2)}) copy-start(bf16[2,2,512,256]{3,2,1,0:T(8,128)(2,1)} %constant.8.clone.first_ref) | copy-start | bytes 3145732
  57.9 8.5 %collective-permute-start = (f32[16,192,128]{2,1,0:T(8,128)S(1)}, f32[16,192,128]{2,1,0:T(8,128)S(1)}, u32[]{:S(2)}, u32[]{:S(2)}) collective-permute-start(f32[16,192,128]{2,1,0:T(8,128)S(1)} %all_to_all.21.data_ref), channel_id=1, source_target_pairs={{0,1},{1,0},{2,3},{3,2},{4,5},{5,4},{6,7},{7,6},{8,9},{9,8},{10,11... | collective-permute-start | bytes 4718600 | tf_op jit(solution)/shard_map/ppermute | solution.py:248

commit v4 on v3

--- a/solution.py
+++ b/solution.py
@@ -66,27 +66,18 @@
     return high, low
 
 
-def prepare(
-    slides_hbm, cutoffs_hbm, strain_hbm, noise_hbm, out_ref, cut_ref, slide, cutoff, strain, noise, sems
-):
-    pairs = ((slides_hbm, slide), (cutoffs_hbm, cutoff), (strain_hbm, strain), (noise_hbm, noise))
-    copies = [pltpu.make_async_copy(a, b, sems.at[i]) for i, (a, b) in enumerate(pairs)]
-    for copy in copies:
-        copy.start()
+def prepare(slide_ref, strain_ref, noise_ref, out_ref):
     bank = jnp.int32(0)
     for name in BANK:
         bank = bank * 2 + lax.axis_index(name)
     slot = lax.broadcasted_iota(jnp.int32, (4, 128), 0)
     lane = lax.broadcasted_iota(jnp.int32, (4, 128), 1)
     bins = bank * (2 * COLS) + slot * 128 + lane
-    for copy in copies:
-        copy.wait()
-    cut_ref[...] = jnp.full((8, 128), cutoff[0], jnp.int32)
-    angle = ((bins * slide[0]) & (SERIES - 1)).astype(jnp.float32) * (2.0 * np.pi / SERIES)
+    angle = ((bins * slide_ref[0]) & (SERIES - 1)).astype(jnp.float32) * (2.0 * np.pi / SERIES)
     cos, sin = jnp.cos(angle), jnp.sin(angle)
-    data_re = strain[pl.ds(0, 4, stride=2), :]
-    data_im = strain[pl.ds(1, 4, stride=2), :]
-    weight = jnp.concatenate([noise[i : i + 1, :] for i in (0, 2, 1, 3)])
+    data_re = strain_ref[pl.ds(0, 4, stride=2), :]
+    data_im = strain_ref[pl.ds(1, 4, stride=2), :]
+    weight = jnp.concatenate([noise_ref[i : i + 1, :] for i in (0, 2, 1, 3)])
     turned_re = (data_re * cos - data_im * sin) * weight
     turned_im = (data_re * sin + data_im * cos) * weight
     for peer in range(16):
@@ -222,24 +213,14 @@
     vmem = pl.BlockSpec(memory_space=pltpu.VMEM)
     params = pltpu.CompilerParams(vmem_limit_bytes=32 * 1024 * 1024)
     cost = pl.CostEstimate(flops=3 * 537 * 10**6, bytes_accessed=6 * 2**20, transcendentals=0)
-    shard, cut = pl.pallas_call(
+    cut = jnp.broadcast_to(cutoffs[:, None], (8, 128))
+    shard = pl.pallas_call(
         prepare,
-        out_shape=(
-            jax.ShapeDtypeStruct((16, 3, 4, 128), jnp.float32),
-            jax.ShapeDtypeStruct((8, 128), jnp.int32),
-        ),
-        in_specs=[pl.BlockSpec(memory_space=pltpu.HBM)] * 4,
-        out_specs=(vmem, vmem),
-        scratch_shapes=[
-            pltpu.SMEM((1,), jnp.int32),
-            pltpu.SMEM((1,), jnp.int32),
-            pltpu.VMEM((8, 128), jnp.float32),
-            pltpu.VMEM((4, 128), jnp.float32),
-            pltpu.SemaphoreType.DMA((4,)),
-        ],
+        out_shape=pltpu.VMEM((16, 3, 4, 128), jnp.float32),
+        in_specs=[pl.BlockSpec(memory_space=pltpu.SMEM), vmem, vmem],
+        out_specs=vmem,
     )(
         slides,
-        cutoffs,
         strain.reshape(2, 2, 2, 128).transpose(0, 2, 1, 3).reshape(8, 128),
         inverse_noise.reshape(2, 2, 128).transpose(1, 0, 2).reshape(4, 128),
     )
@@ -262,7 +243,7 @@
     network, loud = pl.pallas_call(
         rest_kernel,
         out_shape=(
-            jax.ShapeDtypeStruct((4, 256, 128), jnp.float32),
+            pltpu.VMEM((4, 256, 128), jnp.float32),
             jax.ShapeDtypeStruct((4, 4, 2, 32, 128), jnp.float32),
         ),
         in_specs=[vmem] * 6,

time: 105 us -> 103 us (0.981)
  blocking collectives: 87.8 us -> 69.3 us
  waiting for transfers between devices: 0.14 us -> 12.4 us
  starting transfers between devices: 5.52 us -> 10.7 us
  Pallas kernels: 7.87 us -> 6.41 us
  local copies, waits for them, and re-layouts: 0.19 us -> 1.6 us
    all_to_all x1 -> x0, blocking collectives: 18.2 us -> none  [shards(): peaks = lax.all_to_all(peak, STACK, 0, 0)]
    all_to_all x0 -> x1, waiting for transfers between devices: none -> 12.4 us  [shards(): peaks = lax.all_to_all(peak, STACK, 0, 0)]
    all_to_all x0 -> x1, starting transfers between devices: none -> 5.17 us  [shards(): peaks = lax.all_to_all(peak, STACK, 0, 0)]
    pallas_call x2, Pallas kernels: 5.05 us -> 3.59 us  [the longest x1 2.82 us: shards(): pl.pallas_call(rest_kernel, out_shape=(pltpu.VMEM((4, 256, 128), jnp.floa...]
  transfers between devices with their start and end apart: 1 -> 2, of which waited for: 1 -> 1; matrix products, arithmetic and copies ran while one was open for 0% -> 1% of each run, Pallas kernels for 3% -> 3%
where the time goes in v4:
time: 103 us
  blocking collectives  69.3 us (67%)
  waiting for transfers between devices  12.4 us (12%)
  starting transfers between devices  10.7 us (10%)
  Pallas kernels  6.41 us (6%)
  between operations  2.05 us (2%)
  local copies, waits for them, and re-layouts  1.6 us (2%)
    all_to_all x1, blocking collectives, shards(): pile = lax.all_to_all(shard, PILE, 0, 0).reshape(192, 128)  27.4 us
    all_to_all x1, blocking collectives, shards(): lax.all_to_all(jnp.broadcast_to(pile[None], (16, 192, 128)), PLANE, 0, 0)  26.9 us
    all_to_all x1, blocking collectives, shards(): swapped = lax.all_to_all(loud.reshape(32, 32, 128), CHIP, 0, 0)  15 us
    all_to_all x1, waiting for transfers between devices, shards(): peaks = lax.all_to_all(peak, STACK, 0, 0)  12.4 us
    ppermute x1, starting transfers between devices, shards(): other = lax.ppermute(mine, 'core', [(0, 1), (1, 0)])  5.52 us
    all_to_all x1, starting transfers between devices, shards(): peaks = lax.all_to_all(peak, STACK, 0, 0)  5.17 us
    pallas_call x1, Pallas kernels, shards(): pl.pallas_call(rest_kernel, out_shape=(pltpu.VMEM((4, 256, 128), jnp.floa...  2.82 us
    pallas_call x1, Pallas kernels, shards(): pl.pallas_call(own_kernel, out_shape=(jax.ShapeDtypeStruct((2, 512, 128),...  2.82 us
  transfers between devices with their start and end apart: 2, of which 1 were waited for; matrix products, arithmetic and copies ran while one was open for 1% of the time, Pallas kernels for 3%

profile of v4, /device:TPU:1, one launch (start us, length us, event | category | flops | bytes accessed | tf_op | source)
XLA Modules:
  0.0 103.1 jit_solution(2886789265418500594)
XLA Ops:
  1.3 0.8 shard_map.95
  2.0 27.4 %all_to_all.20 = f32[16,3,4,128]{3,2,1,0:T(4,128)S(1)} all-to-all(f32[16,3,4,128]{3,2,1,0:T(4,128)S(1)} %shard_map.95), channel_id=1, replica_groups=mesh['x1'=2,'x0'=2,'z2'=2,'z1'=2,'z0'=2,'y1'=2,'y0'=2,'zh'=2,'core'=2] {..., dimensions={0} | all-to-all | bytes 196608 | tf_op jit(solution)/shard_map/all_to_all | solution.py:227
  29.4 0.1 broadcast_in_dim.25
  29.6 0.0 copy-start
  29.6 0.0 copy-start.1
  29.6 0.0 copy-start.2
  29.6 0.0 copy-start.3
  29.6 26.9 %all_to_all.21.data_ref = f32[16,192,128]{2,1,0:T(8,128)S(1)} all-to-all(f32[16,192,128]{2,1,0:T(8,128)S(1)} %broadcast_in_dim.25), channel_id=1, replica_groups=mesh['x1'=2,'x0'=2,'z2'=2,'z1'=2,'z0'=2,'y1'=2,'y0'=2,'zh'=2,'core'=2] {..., dimensions={0} | all-to-all | bytes 3145728 | tf_op jit(solution)/shard_map/all_to_all | solution.py:228
  56.5 5.5 %collective-permute-start = (f32[16,192,128]{2,1,0:T(8,128)S(1)}, f32[16,192,128]{2,1,0:T(8,128)S(1)}, u32[]{:S(2)}, u32[]{:S(2)}) collective-permute-start(f32[16,192,128]{2,1,0:T(8,128)S(1)} %all_to_all.21.data_ref), channel_id=1, source_target_pairs={{0,1},{1,0},{2,3},{3,2},{4,5},{5,4},{6,7},{7,6},{8,9},{9,8},{10,11... | collective-permute-start | bytes 4718600 | tf_op jit(solution)/shard_map/ppermute | solution.py:229
  62.7 0.0 copy-done
  62.7 0.0 copy-done.1
  62.7 0.0 copy-done.2
  62.7 0.0 copy-done.3
  62.7 2.8 %shard_map.96 = (f32[2,512,128]{2,1,0:T(8,128)S(1)}, f32[2,2,2,128,128]{4,3,2,1,0:T(8,128)S(1)}) custom-call(s32[8,128]{1,0:T(8,128)S(1)} %broadcast_in_dim.23.cut_ref, f32[4,256,128]{2,1,0:T(8,128)S(1)} %bitcast.26, f32[16,192,128]{2,1,0:T(8,128)S(1)} %all_to_all.21.data_ref, bf16[2,2,512,256]{3,2,1,0:T(8,128)(2,1)S(1)} %copy-done.2, ...), custom_call_target="tpu_custom_call" | custom-call | flops 1611000064 | bytes 6291456 | tf_op jit(solution)/shard_map/pallas_call | solution.py:231
  65.6 0.0 collective-permute-done.data_ref
  65.6 2.8 %shard_map.97 = (f32[4,256,128]{2,1,0:T(8,128)S(1)}, f32[4,4,2,32,128]{4,3,2,1,0:T(8,128)S(1)}) custom-call(f32[2,2,2,128,128]{4,3,2,1,0:T(8,128)S(1)} %get-tuple-element.6.masked, f32[2,512,128]{2,1,0:T(8,128)S(1)} %get-tuple-element.7.carry_ref, f32[16,192,128]{2,1,0:T(8,128)S(1)} %collective-permute-done.data_ref, bf16[2,2,512,256]{3,2,1,0:T(8,128)(2,1)S(1)} %copy-done.2, ...), custom_call_target="tpu_custom_call" | custom-call | flops 1611000064 | bytes 6291456 | tf_op jit(solution)/shard_map/pallas_call | solution.py:243
  68.4 15.0 %all_to_all.22 = f32[32,32,128]{2,1,0:T(8,128)S(1)} all-to-all(f32[32,32,128]{2,1,0:T(8,128)S(1)} %bitcast.25), channel_id=1, replica_groups=mesh['x1'=2,'x0'=2,'z2'=2,'z1'=2,'z0'=2,'y1'=2,'y0'=2,'zh'=2,'core'=2] {..., dimensions={0} | all-to-all | bytes 1048576 | tf_op jit(solution)/shard_map/all_to_all | solution.py:258
  83.5 0.6 broadcast_in_dim.27
  84.1 5.2 %all-to-all-start.3 = ((f32[32,4,128]{2,1,0:T(4,128)}), f32[32,4,128]{2,1,0:T(4,128)S(1)}, u32[]{:S(2)}, u32[]{:S(2)}) async-start(f32[32,4,128]{2,1,0:T(4,128)} %bitcast.13), calls=%async_computation.3 | async-start | bytes 131072 | tf_op jit(solution)/shard_map/all_to_all | solution.py:261
  89.3 0.8 copy.33
  90.1 12.4 %all-to-all-done.3 = f32[32,4,128]{2,1,0:T(4,128)S(1)} async-done(((f32[32,4,128]{2,1,0:T(4,128)}), f32[32,4,128]{2,1,0:T(4,128)S(1)}, u32[]{:S(2)}, u32[]{:S(2)}) %all-to-all-start.3) | async-done | bytes 65568 | tf_op jit(solution)/shard_map/all_to_all | solution.py:261
  102.5 0.6 reduce_max.19
  (2 shorter events, 0.0 us)
Async XLA Ops:
  29.6 33.1 %copy-start = (f32[1,256,2,256]{3,2,1,0:T(2,128)S(1)}, f32[1,256,2,256]{3,2,1,0:T(2,128)}, u32[]{:S(2)}) copy-start(f32[1,256,2,256]{3,2,1,0:T(2,128)} %param.11) | copy-start | bytes 1572868
  29.6 33.1 %copy-start.1 = (f32[2,512,256]{2,1,0:T(8,128)S(1)}, f32[2,512,256]{2,1,0:T(8,128)}, u32[]{:S(2)}) copy-start(f32[2,512,256]{2,1,0:T(8,128)} %constant.9.clone.turn_ref) | copy-start | bytes 3145732
  29.6 33.1 %copy-start.2 = (bf16[2,2,512,256]{3,2,1,0:T(8,128)(2,1)S(1)}, bf16[2,2,512,256]{3,2,1,0:T(8,128)(2,1)}, u32[]{:S(2)}) copy-start(bf16[2,2,512,256]{3,2,1,0:T(8,128)(2,1)} %constant.8.clone.first_ref) | copy-start | bytes 3145732
  29.6 33.1 %copy-start.3 = (bf16[2,2,256,256]{3,2,1,0:T(8,128)(2,1)S(1)}, bf16[2,2,256,256]{3,2,1,0:T(8,128)(2,1)}, u32[]{:S(2)}) copy-start(bf16[2,2,256,256]{3,2,1,0:T(8,128)(2,1)} %constant.10.clone.last_ref) | copy-start | bytes 1572868
  56.5 9.1 %collective-permute-start = (f32[16,192,128]{2,1,0:T(8,128)S(1)}, f32[16,192,128]{2,1,0:T(8,128)S(1)}, u32[]{:S(2)}, u32[]{:S(2)}) collective-permute-start(f32[16,192,128]{2,1,0:T(8,128)S(1)} %all_to_all.21.data_ref), channel_id=1, source_target_pairs={{0,1},{1,0},{2,3},{3,2},{4,5},{5,4},{6,7},{7,6},{8,9},{9,8},{10,11... | collective-permute-start | bytes 4718600 | tf_op jit(solution)/shard_map/ppermute | solution.py:229
  84.1 18.4 %all-to-all-start.3 = ((f32[32,4,128]{2,1,0:T(4,128)}), f32[32,4,128]{2,1,0:T(4,128)S(1)}, u32[]{:S(2)}, u32[]{:S(2)}) async-start(f32[32,4,128]{2,1,0:T(4,128)} %bitcast.13), calls=%async_computation.3 | async-start | bytes 131072 | tf_op jit(solution)/shard_map/all_to_all | solution.py:261

commit v5 on v4

--- a/solution.py
+++ b/solution.py
@@ -27,8 +27,8 @@
 
 
 def slot_rows(slot):
-    x = slot // 64 * 2 + slot // 16 % 2
-    y = slot // 32 % 2 * 2 + slot // 8 % 2
+    x = 3 - slot // 64 * 2 - slot // 16 % 2
+    y = 3 - slot // 32 % 2 * 2 - slot // 8 % 2
     return x * 64 + slot % 8 * 8 + y * 2
 
 
@@ -203,7 +203,8 @@
         value = (total[parity, place : place + 128, :] + power).T.reshape(4, 4, 8, 128)
         for y in range(4):
             network_ref[:, pl.ds(y * 8 + parity * 4 + block, 8, stride=32), :] = value[:, y]
-            loud_ref[:, y, parity, pl.ds(block, 8, stride=4), :] = value[:, y]
+            for x in range(4):
+                loud_ref[3 - x, 3 - y, parity, pl.ds(block, 8, stride=4), :] = value[x, y]
 
     pipeline(data_ref, masked, first_ref, turn_ref, last_ref, piece, (more, close))
 
@@ -224,8 +225,10 @@
         strain.reshape(2, 2, 2, 128).transpose(0, 2, 1, 3).reshape(8, 128),
         inverse_noise.reshape(2, 2, 128).transpose(1, 0, 2).reshape(4, 128),
     )
-    pile = lax.all_to_all(shard, PILE, 0, 0).reshape(192, 128)
-    mine = lax.all_to_all(jnp.broadcast_to(pile[None], (16, 192, 128)), PLANE, 0, 0)
+    pile = lax.all_to_all(
+        shard, PILE, 0, 0, axis_index_groups=[list(range(8, 16)) + list(range(8))]
+    ).reshape(192, 128)
+    mine = lax.all_to_all(jnp.broadcast_to(pile[None], (16, 192, 128)), PLANE, 0, 0, axis_index_groups=[list(range(15, -1, -1))])
     other = lax.ppermute(mine, "core", [(0, 1), (1, 0)])
     waves = templates.reshape(ROWS, 2, 2, 128).transpose(0, 2, 1, 3).reshape(4, 256, 128)
     carry, masked = pl.pallas_call(
@@ -255,10 +258,10 @@
         compiler_params=params,
         cost_estimate=cost,
     )(masked, carry, other, first, turn, last)
-    swapped = lax.all_to_all(loud.reshape(32, 32, 128), CHIP, 0, 0)
-    peak = jnp.max(swapped, axis=0).reshape(8, 1, 4, 128)
+    swapped = lax.all_to_all(loud.reshape(32, 32, 128), CHIP, 0, 0, axis_index_groups=[list(range(31, -1, -1))])
+    peak = jnp.max(swapped, axis=0).reshape(8, 1, 4, 128)[::-1]
     peak = jnp.broadcast_to(peak, (8, 4, 4, 128)).reshape(32, 4, 128)
-    peaks = lax.all_to_all(peak, STACK, 0, 0)
+    peaks = lax.all_to_all(peak, STACK, 0, 0, axis_index_groups=[list(range(31, -1, -1))])
     loudest = jnp.max(peaks.reshape(16, 2, 4, 128), axis=0).reshape(1024)
     return (loudest, network.reshape(1, SERIES))
 

time: 103 us -> 99.3 us (0.964)
  blocking collectives: 69.3 us -> 64.2 us
  starting transfers between devices: 10.7 us -> 14.8 us
  waiting for transfers between devices: 12.4 us -> 9.2 us
    all_to_all x3, blocking collectives: 69.3 us -> 64.2 us  [the longest x1 24.9 us: shards(): lax.all_to_all(jnp.broadcast_to(pile[None], (16, 192, 128)), PLANE, 0, 0,...]
    all_to_all x1, starting transfers between devices: 5.17 us -> 10.2 us  [shards(): lax.all_to_all(peak, STACK, 0, 0, axis_index_groups=[list(range(31, -1, -...]
    all_to_all x1, waiting for transfers between devices: 12.4 us -> 9.19 us  [shards(): lax.all_to_all(peak, STACK, 0, 0, axis_index_groups=[list(range(31, -1, -...]
where the time goes in v5:
time: 99.3 us; the launch traced here: 99 us
  blocking collectives  64.2 us (65%)
  starting transfers between devices  14.8 us (15%)
  waiting for transfers between devices  9.2 us (9%)
  Pallas kernels  6.42 us (6%)
  between operations  2.06 us (2%)
  local copies, waits for them, and re-layouts  1.6 us (2%)
    all_to_all x1, blocking collectives, shards(): lax.all_to_all(jnp.broadcast_to(pile[None], (16, 192, 128)), PLANE, 0, 0,...  24.9 us
    all_to_all x1, blocking collectives, shards(): lax.all_to_all(shard, PILE, 0, 0, axis_index_groups=[list(range(8, 16)) +...  24 us
    all_to_all x1, blocking collectives, shards(): lax.all_to_all(loud.reshape(32, 32, 128), CHIP, 0, 0, axis_index_groups=[...  15.2 us
    all_to_all x1, starting transfers between devices, shards(): lax.all_to_all(peak, STACK, 0, 0, axis_index_groups=[list(range(31, -1, -...  10.2 us
    all_to_all x1, waiting for transfers between devices, shards(): lax.all_to_all(peak, STACK, 0, 0, axis_index_groups=[list(range(31, -1, -...  9.19 us
    ppermute x1, starting transfers between devices, shards(): other = lax.ppermute(mine, 'core', [(0, 1), (1, 0)])  4.56 us
    pallas_call x1, Pallas kernels, shards(): pl.pallas_call(own_kernel, out_shape=(jax.ShapeDtypeStruct((2, 512, 128),...  2.83 us
    pallas_call x1, Pallas kernels, shards(): pl.pallas_call(rest_kernel, out_shape=(pltpu.VMEM((4, 256, 128), jnp.floa...  2.83 us
  transfers between devices with their start and end apart: 2, of which 1 were waited for; matrix products, arithmetic and copies ran while one was open for 1% of the time, Pallas kernels for 3%

profile of v5, /device:TPU:1, one launch (start us, length us, event | category | flops | bytes accessed | tf_op | source)
XLA Modules:
  0.0 99.0 jit_solution(17054483369734475592)
XLA Ops:
  1.3 0.8 shard_map.95
  2.0 24.0 %all_to_all.20 = f32[16,3,4,128]{3,2,1,0:T(4,128)S(1)} all-to-all(f32[16,3,4,128]{3,2,1,0:T(4,128)S(1)} %shard_map.95), channel_id=1, replica_groups={{2,18,34,50,66,82,98,114,0,16,32,48,64,80,96,112},{3,19,35,51,67,83,99,..., dimensions={0} | all-to-all | bytes 196608 | tf_op jit(solution)/shard_map/all_to_all | solution.py:228
  26.1 0.1 broadcast_in_dim.25
  26.2 0.0 copy-start
  26.3 0.0 copy-start.1
  26.3 0.0 copy-start.2
  26.3 0.0 copy-start.3
  26.3 24.9 %all_to_all.21.data_ref = f32[16,192,128]{2,1,0:T(8,128)S(1)} all-to-all(f32[16,192,128]{2,1,0:T(8,128)S(1)} %broadcast_in_dim.25), channel_id=1, replica_groups={{396,392,268,264,388,384,260,256,140,136,12,8,132,128,4,0},{397,393,269..., dimensions={0} | all-to-all | bytes 3145728 | tf_op jit(solution)/shard_map/all_to_all | solution.py:231
  51.2 4.6 %collective-permute-start = (f32[16,192,128]{2,1,0:T(8,128)S(1)}, f32[16,192,128]{2,1,0:T(8,128)S(1)}, u32[]{:S(2)}, u32[]{:S(2)}) collective-permute-start(f32[16,192,128]{2,1,0:T(8,128)S(1)} %all_to_all.21.data_ref), channel_id=1, source_target_pairs={{0,1},{1,0},{2,3},{3,2},{4,5},{5,4},{6,7},{7,6},{8,9},{9,8},{10,11... | collective-permute-start | bytes 4718600 | tf_op jit(solution)/shard_map/ppermute | solution.py:232
  56.5 0.0 copy-done
  56.5 0.0 copy-done.1
  56.5 0.0 copy-done.2
  56.5 0.0 copy-done.3
  56.5 2.8 %shard_map.96 = (f32[2,512,128]{2,1,0:T(8,128)S(1)}, f32[2,2,2,128,128]{4,3,2,1,0:T(8,128)S(1)}) custom-call(s32[8,128]{1,0:T(8,128)S(1)} %broadcast_in_dim.23.cut_ref, f32[4,256,128]{2,1,0:T(8,128)S(1)} %bitcast.28, f32[16,192,128]{2,1,0:T(8,128)S(1)} %all_to_all.21.data_ref, bf16[2,2,512,256]{3,2,1,0:T(8,128)(2,1)S(1)} %copy-done.2, ...), custom_call_target="tpu_custom_call" | custom-call | flops 1611000064 | bytes 6291456 | tf_op jit(solution)/shard_map/pallas_call | solution.py:234
  59.3 0.0 collective-permute-done.data_ref
  59.3 2.8 %shard_map.97 = (f32[4,256,128]{2,1,0:T(8,128)S(1)}, f32[4,4,2,32,128]{4,3,2,1,0:T(8,128)S(1)}) custom-call(f32[2,2,2,128,128]{4,3,2,1,0:T(8,128)S(1)} %get-tuple-element.6.masked, f32[2,512,128]{2,1,0:T(8,128)S(1)} %get-tuple-element.7.carry_ref, f32[16,192,128]{2,1,0:T(8,128)S(1)} %collective-permute-done.data_ref, bf16[2,2,512,256]{3,2,1,0:T(8,128)(2,1)S(1)} %copy-done.2, ...), custom_call_target="tpu_custom_call" | custom-call | flops 1611000064 | bytes 6291456 | tf_op jit(solution)/shard_map/pallas_call | solution.py:246
  62.2 15.2 %all_to_all.22 = f32[32,32,128]{2,1,0:T(8,128)S(1)} all-to-all(f32[32,32,128]{2,1,0:T(8,128)S(1)} %bitcast.27), channel_id=1, replica_groups={{397,396,393,392,389,388,385,384,269,268,265,264,261,260,257,256,141,14..., dimensions={0} | all-to-all | bytes 1048576 | tf_op jit(solution)/shard_map/all_to_all | solution.py:261
  77.5 0.6 broadcast_in_dim.27
  78.1 10.2 %all-to-all-start.3 = ((f32[32,4,128]{2,1,0:T(4,128)}), f32[32,4,128]{2,1,0:T(4,128)S(1)}, u32[]{:S(2)}, u32[]{:S(2)}) async-start(f32[32,4,128]{2,1,0:T(4,128)} %bitcast.14), calls=%async_computation.3 | async-start | bytes 131072 | tf_op jit(solution)/shard_map/all_to_all | solution.py:264
  88.3 0.8 copy.33
  89.1 9.2 %all-to-all-done.3 = f32[32,4,128]{2,1,0:T(4,128)S(1)} async-done(((f32[32,4,128]{2,1,0:T(4,128)}), f32[32,4,128]{2,1,0:T(4,128)S(1)}, u32[]{:S(2)}, u32[]{:S(2)}) %all-to-all-start.3) | async-done | bytes 65568 | tf_op jit(solution)/shard_map/all_to_all | solution.py:264
  98.3 0.6 reduce_max.19
  (3 shorter events, 0.1 us)
Async XLA Ops:
  26.2 30.2 %copy-start = (f32[1,256,2,256]{3,2,1,0:T(2,128)S(1)}, f32[1,256,2,256]{3,2,1,0:T(2,128)}, u32[]{:S(2)}) copy-start(f32[1,256,2,256]{3,2,1,0:T(2,128)} %param.11) | copy-start | bytes 1572868
  26.3 30.2 %copy-start.1 = (f32[2,512,256]{2,1,0:T(8,128)S(1)}, f32[2,512,256]{2,1,0:T(8,128)}, u32[]{:S(2)}) copy-start(f32[2,512,256]{2,1,0:T(8,128)} %constant.9.clone.turn_ref) | copy-start | bytes 3145732
  26.3 30.2 %copy-start.2 = (bf16[2,2,512,256]{3,2,1,0:T(8,128)(2,1)S(1)}, bf16[2,2,512,256]{3,2,1,0:T(8,128)(2,1)}, u32[]{:S(2)}) copy-start(bf16[2,2,512,256]{3,2,1,0:T(8,128)(2,1)} %constant.8.clone.first_ref) | copy-start | bytes 3145732
  26.3 30.2 %copy-start.3 = (bf16[2,2,256,256]{3,2,1,0:T(8,128)(2,1)S(1)}, bf16[2,2,256,256]{3,2,1,0:T(8,128)(2,1)}, u32[]{:S(2)}) copy-start(bf16[2,2,256,256]{3,2,1,0:T(8,128)(2,1)} %constant.10.clone.last_ref) | copy-start | bytes 1572868
  51.2 8.1 %collective-permute-start = (f32[16,192,128]{2,1,0:T(8,128)S(1)}, f32[16,192,128]{2,1,0:T(8,128)S(1)}, u32[]{:S(2)}, u32[]{:S(2)}) collective-permute-start(f32[16,192,128]{2,1,0:T(8,128)S(1)} %all_to_all.21.data_ref), channel_id=1, source_target_pairs={{0,1},{1,0},{2,3},{3,2},{4,5},{5,4},{6,7},{7,6},{8,9},{9,8},{10,11... | collective-permute-start | bytes 4718600 | tf_op jit(solution)/shard_map/ppermute | solution.py:232
  78.1 20.2 %all-to-all-start.3 = ((f32[32,4,128]{2,1,0:T(4,128)}), f32[32,4,128]{2,1,0:T(4,128)S(1)}, u32[]{:S(2)}, u32[]{:S(2)}) async-start(f32[32,4,128]{2,1,0:T(4,128)} %bitcast.14), calls=%async_computation.3 | async-start | bytes 131072 | tf_op jit(solution)/shard_map/all_to_all | solution.py:264

commit v6 on v5

--- a/solution.py
+++ b/solution.py
@@ -204,7 +204,7 @@
         for y in range(4):
             network_ref[:, pl.ds(y * 8 + parity * 4 + block, 8, stride=32), :] = value[:, y]
             for x in range(4):
-                loud_ref[3 - x, 3 - y, parity, pl.ds(block, 8, stride=4), :] = value[x, y]
+                loud_ref[3 - x, 3 - y, 1 - parity, pl.ds(block, 8, stride=4), :] = value[x, y]
 
     pipeline(data_ref, masked, first_ref, turn_ref, last_ref, piece, (more, close))
 
@@ -259,9 +259,9 @@
         cost_estimate=cost,
     )(masked, carry, other, first, turn, last)
     swapped = lax.all_to_all(loud.reshape(32, 32, 128), CHIP, 0, 0, axis_index_groups=[list(range(31, -1, -1))])
-    peak = jnp.max(swapped, axis=0).reshape(8, 1, 4, 128)[::-1]
-    peak = jnp.broadcast_to(peak, (8, 4, 4, 128)).reshape(32, 4, 128)
-    peaks = lax.all_to_all(peak, STACK, 0, 0, axis_index_groups=[list(range(31, -1, -1))])
+    peak = jnp.max(swapped, axis=0).reshape(8, 1, 4, 128)
+    peak = jnp.broadcast_to(peak, (2, 8, 2, 4, 128)).reshape(32, 4, 128)
+    peaks = lax.all_to_all(peak, STACK, 0, 0, axis_index_groups=[[z * 4 + h * 2 + c for h in (1, 0) for z in range(8) for c in (0, 1)]])
     loudest = jnp.max(peaks.reshape(16, 2, 4, 128), axis=0).reshape(1024)
     return (loudest, network.reshape(1, SERIES))
 

time: 99.3 us -> 95.8 us (0.965)
  waiting for transfers between devices: 9.2 us -> 3.55 us
  starting transfers between devices: 14.8 us -> 17 us
    all_to_all x1, waiting for transfers between devices: 9.19 us -> 3.55 us  [shards(): lax.all_to_all(peak, STACK, 0, 0, axis_index_groups=[[z * 4 + h * 2 + c f...]
    all_to_all x1, starting transfers between devices: 10.2 us -> 12.4 us  [shards(): lax.all_to_all(peak, STACK, 0, 0, axis_index_groups=[[z * 4 + h * 2 + c f...]
where the time goes in v6:
time: 95.8 us; the launch traced here: 95.4 us
  blocking collectives  64.2 us (67%)
  starting transfers between devices  17 us (18%)
  Pallas kernels  6.42 us (7%)
  waiting for transfers between devices  3.55 us (4%)
  between operations  2.05 us (2%)
  local copies, waits for them, and re-layouts  1.6 us (2%)
    all_to_all x1, blocking collectives, shards(): lax.all_to_all(jnp.broadcast_to(pile[None], (16, 192, 128)), PLANE, 0, 0,...  24.9 us
    all_to_all x1, blocking collectives, shards(): lax.all_to_all(shard, PILE, 0, 0, axis_index_groups=[list(range(8, 16)) +...  24 us
    all_to_all x1, blocking collectives, shards(): lax.all_to_all(loud.reshape(32, 32, 128), CHIP, 0, 0, axis_index_groups=[...  15.2 us
    all_to_all x1, starting transfers between devices, shards(): lax.all_to_all(peak, STACK, 0, 0, axis_index_groups=[[z * 4 + h * 2 + c f...  12.4 us
    ppermute x1, starting transfers between devices, shards(): other = lax.ppermute(mine, 'core', [(0, 1), (1, 0)])  4.56 us
    all_to_all x1, waiting for transfers between devices, shards(): lax.all_to_all(peak, STACK, 0, 0, axis_index_groups=[[z * 4 + h * 2 + c f...  3.55 us
    pallas_call x1, Pallas kernels, shards(): pl.pallas_call(own_kernel, out_shape=(jax.ShapeDtypeStruct((2, 512, 128),...  2.83 us
    pallas_call x1, Pallas kernels, shards(): pl.pallas_call(rest_kernel, out_shape=(pltpu.VMEM((4, 256, 128), jnp.floa...  2.83 us
  transfers between devices with their start and end apart: 2, of which 1 were waited for; matrix products, arithmetic and copies ran while one was open for 1% of the time, Pallas kernels for 3%

profile of v6, /device:TPU:1, one launch (start us, length us, event | category | flops | bytes accessed | tf_op | source)
XLA Modules:
  0.0 95.4 jit_solution(16211365289363757322)
XLA Ops:
  1.3 0.8 shard_map.95
  2.0 24.0 %all_to_all.20 = f32[16,3,4,128]{3,2,1,0:T(4,128)S(1)} all-to-all(f32[16,3,4,128]{3,2,1,0:T(4,128)S(1)} %shard_map.95), channel_id=1, replica_groups={{2,18,34,50,66,82,98,114,0,16,32,48,64,80,96,112},{3,19,35,51,67,83,99,..., dimensions={0} | all-to-all | bytes 196608 | tf_op jit(solution)/shard_map/all_to_all | solution.py:228
  26.1 0.1 broadcast_in_dim.23
  26.2 0.0 copy-start
  26.3 0.0 copy-start.1
  26.3 0.0 copy-start.2
  26.3 0.0 copy-start.3
  26.3 24.9 %all_to_all.21.data_ref = f32[16,192,128]{2,1,0:T(8,128)S(1)} all-to-all(f32[16,192,128]{2,1,0:T(8,128)S(1)} %broadcast_in_dim.23), channel_id=1, replica_groups={{396,392,268,264,388,384,260,256,140,136,12,8,132,128,4,0},{397,393,269..., dimensions={0} | all-to-all | bytes 3145728 | tf_op jit(solution)/shard_map/all_to_all | solution.py:231
  51.2 4.6 %collective-permute-start = (f32[16,192,128]{2,1,0:T(8,128)S(1)}, f32[16,192,128]{2,1,0:T(8,128)S(1)}, u32[]{:S(2)}, u32[]{:S(2)}) collective-permute-start(f32[16,192,128]{2,1,0:T(8,128)S(1)} %all_to_all.21.data_ref), channel_id=1, source_target_pairs={{0,1},{1,0},{2,3},{3,2},{4,5},{5,4},{6,7},{7,6},{8,9},{9,8},{10,11... | collective-permute-start | bytes 4718600 | tf_op jit(solution)/shard_map/ppermute | solution.py:232
  56.5 0.0 copy-done
  56.5 0.0 copy-done.1
  56.5 0.0 copy-done.2
  56.5 0.0 copy-done.3
  56.5 2.8 %shard_map.96 = (f32[2,512,128]{2,1,0:T(8,128)S(1)}, f32[2,2,2,128,128]{4,3,2,1,0:T(8,128)S(1)}) custom-call(s32[8,128]{1,0:T(8,128)S(1)} %broadcast_in_dim.21.cut_ref, f32[4,256,128]{2,1,0:T(8,128)S(1)} %bitcast.26, f32[16,192,128]{2,1,0:T(8,128)S(1)} %all_to_all.21.data_ref, bf16[2,2,512,256]{3,2,1,0:T(8,128)(2,1)S(1)} %copy-done.2, ...), custom_call_target="tpu_custom_call" | custom-call | flops 1611000064 | bytes 6291456 | tf_op jit(solution)/shard_map/pallas_call | solution.py:234
  59.3 0.0 collective-permute-done.data_ref
  59.3 2.8 %shard_map.97 = (f32[4,256,128]{2,1,0:T(8,128)S(1)}, f32[4,4,2,32,128]{4,3,2,1,0:T(8,128)S(1)}) custom-call(f32[2,2,2,128,128]{4,3,2,1,0:T(8,128)S(1)} %get-tuple-element.6.masked, f32[2,512,128]{2,1,0:T(8,128)S(1)} %get-tuple-element.7.carry_ref, f32[16,192,128]{2,1,0:T(8,128)S(1)} %collective-permute-done.data_ref, bf16[2,2,512,256]{3,2,1,0:T(8,128)(2,1)S(1)} %copy-done.2, ...), custom_call_target="tpu_custom_call" | custom-call | flops 1611000064 | bytes 6291456 | tf_op jit(solution)/shard_map/pallas_call | solution.py:246
  62.2 15.2 %all_to_all.22 = f32[32,32,128]{2,1,0:T(8,128)S(1)} all-to-all(f32[32,32,128]{2,1,0:T(8,128)S(1)} %bitcast.25), channel_id=1, replica_groups={{397,396,393,392,389,388,385,384,269,268,265,264,261,260,257,256,141,14..., dimensions={0} | all-to-all | bytes 1048576 | tf_op jit(solution)/shard_map/all_to_all | solution.py:261
  77.5 0.6 broadcast_in_dim.24
  78.1 12.4 %all-to-all-start.3 = ((f32[32,4,128]{2,1,0:T(4,128)}), f32[32,4,128]{2,1,0:T(4,128)S(1)}, u32[]{:S(2)}, u32[]{:S(2)}) async-start(f32[32,4,128]{2,1,0:T(4,128)} %bitcast.13), calls=%async_computation.3 | async-start | bytes 131072 | tf_op jit(solution)/shard_map/all_to_all | solution.py:264
  90.5 0.8 copy.33
  91.3 3.5 %all-to-all-done.3 = f32[32,4,128]{2,1,0:T(4,128)S(1)} async-done(((f32[32,4,128]{2,1,0:T(4,128)}), f32[32,4,128]{2,1,0:T(4,128)S(1)}, u32[]{:S(2)}, u32[]{:S(2)}) %all-to-all-start.3) | async-done | bytes 65568 | tf_op jit(solution)/shard_map/all_to_all | solution.py:264
  94.8 0.6 reduce_max.19
  (2 shorter events, 0.0 us)
Async XLA Ops:
  26.2 30.2 %copy-start = (f32[1,256,2,256]{3,2,1,0:T(2,128)S(1)}, f32[1,256,2,256]{3,2,1,0:T(2,128)}, u32[]{:S(2)}) copy-start(f32[1,256,2,256]{3,2,1,0:T(2,128)} %param.11) | copy-start | bytes 1572868
  26.3 30.2 %copy-start.1 = (f32[2,512,256]{2,1,0:T(8,128)S(1)}, f32[2,512,256]{2,1,0:T(8,128)}, u32[]{:S(2)}) copy-start(f32[2,512,256]{2,1,0:T(8,128)} %constant.9.clone.turn_ref) | copy-start | bytes 3145732
  26.3 30.2 %copy-start.2 = (bf16[2,2,512,256]{3,2,1,0:T(8,128)(2,1)S(1)}, bf16[2,2,512,256]{3,2,1,0:T(8,128)(2,1)}, u32[]{:S(2)}) copy-start(bf16[2,2,512,256]{3,2,1,0:T(8,128)(2,1)} %constant.8.clone.first_ref) | copy-start | bytes 3145732
  26.3 30.2 %copy-start.3 = (bf16[2,2,256,256]{3,2,1,0:T(8,128)(2,1)S(1)}, bf16[2,2,256,256]{3,2,1,0:T(8,128)(2,1)}, u32[]{:S(2)}) copy-start(bf16[2,2,256,256]{3,2,1,0:T(8,128)(2,1)} %constant.10.clone.last_ref) | copy-start | bytes 1572868
  51.2 8.1 %collective-permute-start = (f32[16,192,128]{2,1,0:T(8,128)S(1)}, f32[16,192,128]{2,1,0:T(8,128)S(1)}, u32[]{:S(2)}, u32[]{:S(2)}) collective-permute-start(f32[16,192,128]{2,1,0:T(8,128)S(1)} %all_to_all.21.data_ref), channel_id=1, source_target_pairs={{0,1},{1,0},{2,3},{3,2},{4,5},{5,4},{6,7},{7,6},{8,9},{9,8},{10,11... | collective-permute-start | bytes 4718600 | tf_op jit(solution)/shard_map/ppermute | solution.py:232
  78.1 16.7 %all-to-all-start.3 = ((f32[32,4,128]{2,1,0:T(4,128)}), f32[32,4,128]{2,1,0:T(4,128)S(1)}, u32[]{:S(2)}, u32[]{:S(2)}) async-start(f32[32,4,128]{2,1,0:T(4,128)} %bitcast.13), calls=%async_computation.3 | async-start | bytes 131072 | tf_op jit(solution)/shard_map/all_to_all | solution.py:264

commit v7 on v6

--- a/solution.py
+++ b/solution.py
@@ -27,8 +27,8 @@
 
 
 def slot_rows(slot):
-    x = 3 - slot // 64 * 2 - slot // 16 % 2
-    y = 3 - slot // 32 % 2 * 2 - slot // 8 % 2
+    x = 2 - slot // 64 * 2 + slot // 16 % 2
+    y = 2 - slot // 32 % 2 * 2 + slot // 8 % 2
     return x * 64 + slot % 8 * 8 + y * 2
 
 
@@ -204,7 +204,7 @@
         for y in range(4):
             network_ref[:, pl.ds(y * 8 + parity * 4 + block, 8, stride=32), :] = value[:, y]
             for x in range(4):
-                loud_ref[3 - x, 3 - y, 1 - parity, pl.ds(block, 8, stride=4), :] = value[x, y]
+                loud_ref[x ^ 2, y ^ 2, parity, pl.ds(block, 8, stride=4), :] = value[x, y]
 
     pipeline(data_ref, masked, first_ref, turn_ref, last_ref, piece, (more, close))
 
@@ -228,7 +228,7 @@
     pile = lax.all_to_all(
         shard, PILE, 0, 0, axis_index_groups=[list(range(8, 16)) + list(range(8))]
     ).reshape(192, 128)
-    mine = lax.all_to_all(jnp.broadcast_to(pile[None], (16, 192, 128)), PLANE, 0, 0, axis_index_groups=[list(range(15, -1, -1))])
+    mine = lax.all_to_all(jnp.broadcast_to(pile[None], (16, 192, 128)), PLANE, 0, 0, axis_index_groups=[[i ^ 12 for i in range(16)]])
     other = lax.ppermute(mine, "core", [(0, 1), (1, 0)])
     waves = templates.reshape(ROWS, 2, 2, 128).transpose(0, 2, 1, 3).reshape(4, 256, 128)
     carry, masked = pl.pallas_call(
@@ -258,7 +258,7 @@
         compiler_params=params,
         cost_estimate=cost,
     )(masked, carry, other, first, turn, last)
-    swapped = lax.all_to_all(loud.reshape(32, 32, 128), CHIP, 0, 0, axis_index_groups=[list(range(31, -1, -1))])
+    swapped = lax.all_to_all(loud.reshape(32, 32, 128), CHIP, 0, 0, axis_index_groups=[[i ^ 20 for i in range(32)]])
     peak = jnp.max(swapped, axis=0).reshape(8, 1, 4, 128)
     peak = jnp.broadcast_to(peak, (2, 8, 2, 4, 128)).reshape(32, 4, 128)
     peaks = lax.all_to_all(peak, STACK, 0, 0, axis_index_groups=[[z * 4 + h * 2 + c for h in (1, 0) for z in range(8) for c in (0, 1)]])

time: 95.8 us -> 94.6 us (0.987)
  blocking collectives: 64.2 us -> 63 us
    all_to_all x1, blocking collectives: 15.2 us -> 14.1 us  [shards(): lax.all_to_all(loud.reshape(32, 32, 128), CHIP, 0, 0, axis_index_groups=[...]
where the time goes in v7:
time: 94.6 us; the launch traced here: 94.3 us
  blocking collectives  63 us (67%)
  starting transfers between devices  17 us (18%)
  Pallas kernels  6.41 us (7%)
  waiting for transfers between devices  3.55 us (4%)
  between operations  2.05 us (2%)
  local copies, waits for them, and re-layouts  1.6 us (2%)
    all_to_all x1, blocking collectives, shards(): lax.all_to_all(jnp.broadcast_to(pile[None], (16, 192, 128)), PLANE, 0, 0,...  24.8 us
    all_to_all x1, blocking collectives, shards(): lax.all_to_all(shard, PILE, 0, 0, axis_index_groups=[list(range(8, 16)) +...  24 us
    all_to_all x1, blocking collectives, shards(): lax.all_to_all(loud.reshape(32, 32, 128), CHIP, 0, 0, axis_index_groups=[...  14.1 us
    all_to_all x1, starting transfers between devices, shards(): lax.all_to_all(peak, STACK, 0, 0, axis_index_groups=[[z * 4 + h * 2 + c f...  12.2 us
    ppermute x1, starting transfers between devices, shards(): other = lax.ppermute(mine, 'core', [(0, 1), (1, 0)])  4.79 us
    all_to_all x1, waiting for transfers between devices, shards(): lax.all_to_all(peak, STACK, 0, 0, axis_index_groups=[[z * 4 + h * 2 + c f...  3.55 us
    pallas_call x1, Pallas kernels, shards(): pl.pallas_call(own_kernel, out_shape=(jax.ShapeDtypeStruct((2, 512, 128),...  2.83 us
    pallas_call x1, Pallas kernels, shards(): pl.pallas_call(rest_kernel, out_shape=(pltpu.VMEM((4, 256, 128), jnp.floa...  2.82 us
  transfers between devices with their start and end apart: 2, of which 1 were waited for; matrix products, arithmetic and copies ran while one was open for 1% of the time, Pallas kernels for 3%

profile of v7, /device:TPU:1, one launch (start us, length us, event | category | flops | bytes accessed | tf_op | source)
XLA Modules:
  0.0 94.3 jit_solution(2983793194153664586)
XLA Ops:
  1.3 0.8 shard_map.95
  2.0 24.0 %all_to_all.20 = f32[16,3,4,128]{3,2,1,0:T(4,128)S(1)} all-to-all(f32[16,3,4,128]{3,2,1,0:T(4,128)S(1)} %shard_map.95), channel_id=1, replica_groups={{2,18,34,50,66,82,98,114,0,16,32,48,64,80,96,112},{3,19,35,51,67,83,99,..., dimensions={0} | all-to-all | bytes 196608 | tf_op jit(solution)/shard_map/all_to_all | solution.py:228
  26.1 0.1 broadcast_in_dim.23
  26.2 0.0 copy-start
  26.3 0.0 copy-start.1
  26.3 0.0 copy-start.2
  26.3 0.0 copy-start.3
  26.3 24.8 %all_to_all.21.data_ref = f32[16,192,128]{2,1,0:T(8,128)S(1)} all-to-all(f32[16,192,128]{2,1,0:T(8,128)S(1)} %broadcast_in_dim.23), channel_id=1, replica_groups={{264,268,392,396,256,260,384,388,8,12,136,140,0,4,128,132},{265,269,393..., dimensions={0} | all-to-all | bytes 3145728 | tf_op jit(solution)/shard_map/all_to_all | solution.py:231
  51.1 4.8 %collective-permute-start = (f32[16,192,128]{2,1,0:T(8,128)S(1)}, f32[16,192,128]{2,1,0:T(8,128)S(1)}, u32[]{:S(2)}, u32[]{:S(2)}) collective-permute-start(f32[16,192,128]{2,1,0:T(8,128)S(1)} %all_to_all.21.data_ref), channel_id=1, source_target_pairs={{0,1},{1,0},{2,3},{3,2},{4,5},{5,4},{6,7},{7,6},{8,9},{9,8},{10,11... | collective-permute-start | bytes 4718600 | tf_op jit(solution)/shard_map/ppermute | solution.py:232
  56.5 0.0 copy-done
  56.5 0.0 copy-done.1
  56.6 0.0 copy-done.2
  56.6 0.0 copy-done.3
  56.6 2.8 %shard_map.96 = (f32[2,512,128]{2,1,0:T(8,128)S(1)}, f32[2,2,2,128,128]{4,3,2,1,0:T(8,128)S(1)}) custom-call(s32[8,128]{1,0:T(8,128)S(1)} %broadcast_in_dim.21.cut_ref, f32[4,256,128]{2,1,0:T(8,128)S(1)} %bitcast.26, f32[16,192,128]{2,1,0:T(8,128)S(1)} %all_to_all.21.data_ref, bf16[2,2,512,256]{3,2,1,0:T(8,128)(2,1)S(1)} %copy-done.2, ...), custom_call_target="tpu_custom_call" | custom-call | flops 1611000064 | bytes 6291456 | tf_op jit(solution)/shard_map/pallas_call | solution.py:234
  59.4 0.0 collective-permute-done.data_ref
  59.4 2.8 %shard_map.97 = (f32[4,256,128]{2,1,0:T(8,128)S(1)}, f32[4,4,2,32,128]{4,3,2,1,0:T(8,128)S(1)}) custom-call(f32[2,2,2,128,128]{4,3,2,1,0:T(8,128)S(1)} %get-tuple-element.6.masked, f32[2,512,128]{2,1,0:T(8,128)S(1)} %get-tuple-element.7.carry_ref, f32[16,192,128]{2,1,0:T(8,128)S(1)} %collective-permute-done.data_ref, bf16[2,2,512,256]{3,2,1,0:T(8,128)(2,1)S(1)} %copy-done.2, ...), custom_call_target="tpu_custom_call" | custom-call | flops 1611000064 | bytes 6291456 | tf_op jit(solution)/shard_map/pallas_call | solution.py:246
  62.3 14.1 %all_to_all.22 = f32[32,32,128]{2,1,0:T(8,128)S(1)} all-to-all(f32[32,32,128]{2,1,0:T(8,128)S(1)} %bitcast.25), channel_id=1, replica_groups={{264,265,268,269,256,257,260,261,392,393,396,397,384,385,388,389,8,9,12..., dimensions={0} | all-to-all | bytes 1048576 | tf_op jit(solution)/shard_map/all_to_all | solution.py:261
  76.4 0.6 broadcast_in_dim.24
  77.1 12.2 %all-to-all-start.3 = ((f32[32,4,128]{2,1,0:T(4,128)}), f32[32,4,128]{2,1,0:T(4,128)S(1)}, u32[]{:S(2)}, u32[]{:S(2)}) async-start(f32[32,4,128]{2,1,0:T(4,128)} %bitcast.13), calls=%async_computation.3 | async-start | bytes 131072 | tf_op jit(solution)/shard_map/all_to_all | solution.py:264
  89.3 0.8 copy.33
  90.1 3.5 %all-to-all-done.3 = f32[32,4,128]{2,1,0:T(4,128)S(1)} async-done(((f32[32,4,128]{2,1,0:T(4,128)}), f32[32,4,128]{2,1,0:T(4,128)S(1)}, u32[]{:S(2)}, u32[]{:S(2)}) %all-to-all-start.3) | async-done | bytes 65568 | tf_op jit(solution)/shard_map/all_to_all | solution.py:264
  93.7 0.6 reduce_max.19
  (2 shorter events, 0.0 us)
Async XLA Ops:
  26.2 30.3 %copy-start = (f32[1,256,2,256]{3,2,1,0:T(2,128)S(1)}, f32[1,256,2,256]{3,2,1,0:T(2,128)}, u32[]{:S(2)}) copy-start(f32[1,256,2,256]{3,2,1,0:T(2,128)} %param.11) | copy-start | bytes 1572868
  26.3 30.3 %copy-start.1 = (f32[2,512,256]{2,1,0:T(8,128)S(1)}, f32[2,512,256]{2,1,0:T(8,128)}, u32[]{:S(2)}) copy-start(f32[2,512,256]{2,1,0:T(8,128)} %constant.9.clone.turn_ref) | copy-start | bytes 3145732
  26.3 30.3 %copy-start.2 = (bf16[2,2,512,256]{3,2,1,0:T(8,128)(2,1)S(1)}, bf16[2,2,512,256]{3,2,1,0:T(8,128)(2,1)}, u32[]{:S(2)}) copy-start(bf16[2,2,512,256]{3,2,1,0:T(8,128)(2,1)} %constant.8.clone.first_ref) | copy-start | bytes 3145732
  26.3 30.3 %copy-start.3 = (bf16[2,2,256,256]{3,2,1,0:T(8,128)(2,1)S(1)}, bf16[2,2,256,256]{3,2,1,0:T(8,128)(2,1)}, u32[]{:S(2)}) copy-start(bf16[2,2,256,256]{3,2,1,0:T(8,128)(2,1)} %constant.10.clone.last_ref) | copy-start | bytes 1572868
  51.1 8.3 %collective-permute-start = (f32[16,192,128]{2,1,0:T(8,128)S(1)}, f32[16,192,128]{2,1,0:T(8,128)S(1)}, u32[]{:S(2)}, u32[]{:S(2)}) collective-permute-start(f32[16,192,128]{2,1,0:T(8,128)S(1)} %all_to_all.21.data_ref), channel_id=1, source_target_pairs={{0,1},{1,0},{2,3},{3,2},{4,5},{5,4},{6,7},{7,6},{8,9},{9,8},{10,11... | collective-permute-start | bytes 4718600 | tf_op jit(solution)/shard_map/ppermute | solution.py:232
  77.1 16.6 %all-to-all-start.3 = ((f32[32,4,128]{2,1,0:T(4,128)}), f32[32,4,128]{2,1,0:T(4,128)S(1)}, u32[]{:S(2)}, u32[]{:S(2)}) async-start(f32[32,4,128]{2,1,0:T(4,128)} %bitcast.13), calls=%async_computation.3 | async-start | bytes 131072 | tf_op jit(solution)/shard_map/all_to_all | solution.py:264
